TPU v7x, 128 devices: a whole 4x4x4 slice. The times are simulated.
128 devices in a mesh: ens: 4 (over y), cx: 8 (over x, core), cy: 4 (over z).
Axes of the slice: x: 4, y: 4, z: 4, core: 2. Of those that a mesh axis runs over, the one named last changes fastest.
Arguments:
- conformations: float32 [3, 8, 32768, 128], P(None, 'ens', ('cx', 'cy')), may hold values from -2.8 to 2.8
- fill_counts: int32 [8, 32768], P('ens', ('cx', 'cy')), may hold values from 48 to 128
- dest_slots: int32 [8, 32768], P('ens', ('cx', 'cy')), may hold values from 0 to 1535, as said below
- dest_cells: int32 [8, 32768], P('ens', ('cx', 'cy')), may hold values from 0 to 2047
- velocity: float32 [3, 64, 1024], P(None, 'cx', 'cy'), may hold values from -6 to 6
- noise: float32 [3, 8, 49152, 128], P(None, 'ens', ('cx', 'cy')), may hold values from -6 to 6
Outputs:
- new_conformations: float32 [3, 8, 49152, 128], P(None, 'ens', ('cx', 'cy'))
- new_velocity: float32 [3, 64, 1024], P(None, 'cx', 'cy')
Inputs may be any that keep to these rules, and one draw needn't show every extreme that they name: `dest_slots`: within one group the blocks of one device take different slots; slot k sends a block to owner k // 48 of the joined cx+cy axes. In every group some owner receives 48 blocks from every device. `fill_counts`: the live dumbbells of a block fill its first slots. `dest_cells`: A cell of the receiving owner, numbered x first over its 8 x 4 x 64 cells.
All inputs are finite; a program needn't handle non-finite values.
Results may differ from a plain program's by a relative error of at most 0.0003.
Values sent between devices are 32-bit elements; how exact they have to be, the bound alone decides.
A program may use at most 128 MiB of HBM per device.

v0:
```python
import math

import jax
import jax.numpy as jnp
from jax import lax
from jax.sharding import PartitionSpec as P

DUMB = 64
NZ = 64


PAIR_FIRST = (0, 1, 2, 0, 0, 1)
PAIR_SECOND = (0, 1, 2, 1, 2, 2)
PAIR_INDEX = ((0, 3, 4), (3, 1, 5), (4, 5, 2))
TIME_STEP = 0.02
WEISSENBERG = 0.5
EXTENSION = 50.0
VISCOSITY = 1.0


def extended(block, sides, width):
    for axis, dim in sides:
        count = lax.axis_size(axis)
        forward = [(i, i + 1) for i in range(count - 1)]
        backward = [(target, source) for source, target in forward]
        low = lax.ppermute(
            lax.slice_in_dim(block, block.shape[dim] - width, None, axis=dim), axis, forward
        )
        high = lax.ppermute(lax.slice_in_dim(block, 0, width, axis=dim), axis, backward)
        block = jnp.concatenate([low, block, high], axis=dim)
    return block


def stencil_parts(padded, depth_cells):
    middle = padded[:, 1:-1, depth_cells:-depth_cells]
    east_side = padded[:, 2:, depth_cells:-depth_cells]
    west_side = padded[:, :-2, depth_cells:-depth_cells]
    north_side = padded[:, 1:-1, 2 * depth_cells :]
    south_side = padded[:, 1:-1, : -2 * depth_cells]
    layer_index = jnp.arange(middle.shape[-1], dtype=jnp.int32) % depth_cells
    blank_edge = jnp.zeros_like(middle[..., :1])
    upper_side = jnp.where(
        layer_index < depth_cells - 1, jnp.concatenate([middle[..., 1:], blank_edge], axis=-1), 0.0
    )
    lower_side = jnp.where(
        layer_index > 0, jnp.concatenate([blank_edge, middle[..., :-1]], axis=-1), 0.0
    )
    return (middle, east_side, west_side, north_side, south_side, upper_side, lower_side)


def differences(stencil):
    middle, east_side, west_side, north_side, south_side, upper_side, lower_side = stencil
    return (
        0.5 * (east_side - west_side),
        0.5 * (north_side - south_side),
        0.5 * (upper_side - lower_side),
    )


def momentum(vel_parts, stress_parts):
    middle, east_side, west_side, north_side, south_side, upper_side, lower_side = vel_parts
    laplace = (
        east_side + west_side + north_side + south_side + upper_side + lower_side - 6.0 * middle
    )
    slopes = differences(stress_parts)
    divergence = jnp.stack(
        [
            slopes[0][PAIR_INDEX[component][0]]
            + slopes[1][PAIR_INDEX[component][1]]
            + slopes[2][PAIR_INDEX[component][2]]
            for component in range(3)
        ]
    )
    return middle + TIME_STEP * (VISCOSITY * laplace + divergence)


def with_rims(field_in):
    widened = extended(field_in, (("cx", 1),), 1)
    return extended(widened, (("cy", 2),), NZ)


def on_device(conformations, fill_counts, dest_slots, dest_cells, velocity, noise):
    groups = conformations.shape[1]
    block_count = conformations.shape[2]
    slot_count = conformations.shape[3]
    place_count = noise.shape[2]
    group_rows = jnp.arange(groups, dtype=jnp.int32)[:, None]
    block_ids = jnp.broadcast_to(
        jnp.arange(block_count, dtype=jnp.int32)[None, :], (groups, block_count)
    )
    source_of = (
        jnp.full((groups, place_count), block_count, jnp.int32)
        .at[group_rows, dest_slots]
        .set(block_ids)
    )
    present = source_of < block_count
    flat_rows = (group_rows * block_count + jnp.minimum(source_of, block_count - 1)).reshape(-1)
    flat_states = conformations.reshape(3, groups * block_count, slot_count)
    outgoing = jnp.take(flat_states, flat_rows, axis=1).reshape(3, groups, place_count, slot_count)
    label_rows = jnp.stack([fill_counts, dest_cells]).reshape(2, groups * block_count)
    labels = jnp.where(
        present[None], jnp.take(label_rows, flat_rows, axis=1).reshape(2, groups, place_count), 0
    )
    arrived, tagged = (
        lax.all_to_all(outgoing, ("cx", "cy"), split_axis=2, concat_axis=2, tiled=True),
        lax.all_to_all(labels, ("cx", "cy"), split_axis=2, concat_axis=2, tiled=True),
    )
    fill_at = tagged[0]
    cell_at = tagged[1]
    mask_live = jnp.arange(slot_count, dtype=jnp.int32) < fill_at[..., None]
    placed = jnp.where(mask_live, arrived, 0.0)
    vel_parts = stencil_parts(with_rims(velocity), NZ)
    gradient = jnp.stack(differences(vel_parts), axis=1).reshape(9, -1)
    gradient_at = gradient[:, cell_at]
    square = jnp.sum(placed * placed, axis=0)
    spring = placed / (1.0 - square / EXTENSION)
    stretch = jnp.stack(
        [
            sum(
                (
                    gradient_at[3 * component + partner][..., None] * placed[partner]
                    for partner in range(3)
                )
            )
            for component in range(3)
        ]
    )
    stepped = (
        placed
        + TIME_STEP * (stretch - spring / (2.0 * WEISSENBERG))
        + math.sqrt(TIME_STEP / WEISSENBERG) * noise
    )
    updated = jnp.where(mask_live, stepped, 0.0)
    first_rows = jnp.array(PAIR_FIRST, dtype=jnp.int32)
    second_rows = jnp.array(PAIR_SECOND, dtype=jnp.int32)
    stress = jnp.sum(placed[first_rows] * spring[second_rows], axis=-1) / (WEISSENBERG * DUMB)
    cell_count = velocity.shape[1] * velocity.shape[2]
    cell_ids = jnp.arange(cell_count, dtype=jnp.int32)
    table = (cell_at.reshape(-1)[:, None] == cell_ids[None, :]).astype(jnp.float32)
    partial_sums = jnp.dot(
        stress.reshape(6, groups * place_count),
        table,
        precision=lax.Precision.HIGHEST,
        preferred_element_type=jnp.float32,
    )
    stress_field = lax.psum(partial_sums, "ens")
    stress_parts = stencil_parts(
        with_rims(stress_field.reshape(6, velocity.shape[1], velocity.shape[2])), NZ
    )
    return (updated, momentum(vel_parts, stress_parts))


def solution(mesh):
    placed = (
        P(None, "ens", ("cx", "cy"), None),
        P("ens", ("cx", "cy")),
        P("ens", ("cx", "cy")),
        P("ens", ("cx", "cy")),
        P(None, "cx", "cy"),
        P(None, "ens", ("cx", "cy"), None),
    )
    return jax.shard_map(
        on_device,
        mesh=mesh,
        in_specs=placed,
        out_specs=(P(None, "ens", ("cx", "cy"), None), P(None, "cx", "cy")),
        check_vma=False,
    )
```

profile of v0, /device:TPU:1, one launch (start us, length us, event | category | flops | bytes accessed | tf_op | source)
XLA Modules:
  0.0 280.6 jit_solution(16723007826971367229)
XLA Ops:
  2.9 8.1 %scatter_custom_fusion = s32[3072]{0:T(1024)S(1)} fusion(s32[2048]{0:T(1024)S(1)} %get-tuple-element.46, s32[2048]{0:T(1024)S(1)} %get-tuple-element.45, s32[]{:T(128)} %constant.29.clone.1), kind=kCustom, calls=%fused_computation.93 | custom fusion | bytes 12292
  13.8 8.1 %gather_fusion = s32[3072,2]{1,0:T(8,128)S(1)} fusion(s32[2,2048]{0,1:T(8,128)S(1)} %copy.114, s32[3072]{0:T(1024)S(1)} %broadcast_clamp_fusion.1), kind=kCustom, calls=%fused_computation | custom fusion | bytes 61440 | tf_op jit(solution)/shard_map/jit(_take)/gather | solution.py:102
  22.0 9.7 %copy.115 = s32[2,2,1536]{1,0,2:T(2,128)S(1)} copy(s32[2,2,1536]{0,2,1:T(8,128)S(1)} %bitcast.82) | data formatting | bytes 49152 | tf_op jit(solution)/shard_map/jit(_take)/gather | solution.py:102
  36.3 9.4 %all-to-all-start = ((s32[32,1,192]{2,1,0:T(1,128)}), s32[32,1,192]{2,1,0:T(1,128)S(1)}, u32[]{:S(2)}, u32[]{:S(2)}) async-start(s32[32,1,192]{2,1,0:T(1,128)} %reshape.180), calls=%async_computation | async-start | bytes 65536 | tf_op jit(solution)/shard_map/all_to_all | solution.py:106
  45.7 6.1 %copy.118 = f32[3,2,1024,128]{3,0,2,1:T(4,128)} copy(f32[3,2,1024,128]{3,2,1,0:T(8,128)} %param.8) | data formatting | bytes 6291456 | tf_op args[0]
  51.8 24.9 %gather_fusion.1 = f32[3072,3,128]{2,1,0:T(4,128)} fusion(f32[3,2048,128]{2,0,1:T(4,128)} %bitcast.79, s32[3072]{0:T(1024)S(1)} %broadcast_clamp_fusion.1), kind=kCustom, calls=%fused_computation.1 | custom fusion | bytes 9449472 | tf_op jit(solution)/shard_map/jit(_take)/gather | solution.py:99
  76.7 6.5 %copy_select_fusion = f32[3,2,1536,128]{3,0,1,2:T(4,128)} fusion(f32[3,2,1536,128]{3,0,2,1:T(4,128)} %bitcast.78, pred[2,1536]{0,1:T(8,128)(4,1)S(1)} %copy.113), kind=kLoop, calls=%fused_computation.10 | loop fusion | flops 1179648 | bytes 9440256 | tf_op jit(solution)/shard_map/jit(_take)/select_n | solution.py:99
  83.3 7.6 %all-to-all-start.1 = ((f32[3,2,1536,128]{3,0,1,2:T(4,128)}), f32[3,2,1536,128]{3,0,1,2:T(4,128)}, u32[]{:S(2)}, u32[]{:S(2)}) async-start(f32[3,2,1536,128]{3,0,1,2:T(4,128)} %copy_select_fusion), calls=%async_computation.1 | async-start | bytes 12582912 | tf_op jit(solution)/shard_map/all_to_all | solution.py:105
  90.9 3.5 %collective-permute-start.1 = (f32[3,1,256]{2,1,0:T(1,128)S(1)}, f32[3,1,256]{2,1,0:T(1,128)S(1)}, u32[]{:S(2)}, u32[]{:S(2)}) collective-permute-start(f32[3,1,256]{2,1,0:T(1,128)S(1)} %get-tuple-element.41), channel_id=1, source_target_pairs={{0,4},{4,8},{8,12},{12,16},{16,20},{20,24},{24,28},{1,5},{5,9},{9,... | collective-permute-start | bytes 9224 | tf_op jit(solution)/shard_map/ppermute | solution.py:26
  97.2 62.4 %collective-permute-done.1 = f32[3,1,256]{2,1,0:T(1,128)S(1)} collective-permute-done((f32[3,1,256]{2,1,0:T(1,128)S(1)}, f32[3,1,256]{2,1,0:T(1,128)S(1)}, u32[]{:S(2)}, u32[]{:S(2)}) %collective-permute-start.1) | collective-permute-done | bytes 3104 | tf_op jit(solution)/shard_map/ppermute | solution.py:26
  159.6 8.6 %collective-permute-done = f32[3,1,256]{2,1,0:T(1,128)S(1)} collective-permute-done((f32[3,1,256]{2,1,0:T(1,128)S(1)}, f32[3,1,256]{2,1,0:T(1,128)S(1)}, u32[]{:S(2)}, u32[]{:S(2)}) %collective-permute-start) | collective-permute-done | bytes 3104 | tf_op jit(solution)/shard_map/ppermute | solution.py:29
  171.4 3.1 %collective-permute-done.2 = f32[3,10,64]{2,1,0:T(8,128)S(1)} collective-permute-done((f32[3,10,64]{2,1,0:T(8,128)S(1)}, f32[3,10,64]{2,1,0:T(8,128)S(1)}, u32[]{:S(2)}, u32[]{:S(2)}) %collective-permute-start.2) | collective-permute-done | bytes 7712 | tf_op jit(solution)/shard_map/ppermute | solution.py:29
  183.9 8.1 %gather_fusion.2 = f32[3072,9]{1,0:T(8,128)S(1)} fusion(f32[9,2048]{0,1:T(8,128)S(1)} %copy.123, s32[3072]{0:T(1024)S(1)} %broadcast_clamp_fusion), kind=kCustom, calls=%fused_computation.2 | custom fusion | bytes 233472 | tf_op jit(solution)/shard_map/gather | solution.py:114
  193.2 6.5 %multiply_reduce_fusion.1 = (f32[2,1536,128]{2,1,0:T(8,128)S(1)}, f32[3,2,1536,128]{3,2,1,0:T(8,128)}) fusion(f32[3,2,1536,128]{3,0,1,2:T(4,128)} %all-to-all-done.1, pred[2,1536,128]{2,1,0:T(8,128)(4,1)S(1)} %iota_compare_fusion.2), kind=kLoop, calls=%fused_computation.17 | loop fusion | flops 3145728 | bytes 11403264 | tf_op jit(solution)/shard_map/reduce_sum | solution.py:115
  199.8 7.3 %gather_fusion.3 = f32[6,2,1536,128]{3,2,1,0:T(8,128)} fusion(f32[3,2,1536,128]{3,2,1,0:T(8,128)} %get-tuple-element.9, s32[1024]{0:T(1024)} %pad_clamp_fusion.1), kind=kCustom, calls=%fused_computation.3 | custom fusion | bytes 18874392 | tf_op jit(solution)/shard_map/gather | solution.py:136
  207.1 9.3 %multiply_add_fusion.2 = (f32[1,2,1536,128]{3,2,1,0:T(8,128)S(1)}, f32[1,2,1536,128]{3,2,1,0:T(8,128)S(1)}, f32[1,2,1536,128]{3,2,1,0:T(8,128)S(1)}) fusion(f32[3,2,1536,128]{3,2,1,0:T(8,128)} %get-tuple-element.9, f32[2,1536]{1,0:T(2,128)S(1)} %get-tuple-element.26, f32[2,1536]{1,0:T(2,128)S(1)} %get-tuple-element.27, f32[2,1536]{1,0:T(2,128)S(1)} %get-tuple-element.20, ...), kind=kLoop, calls=%fused_computation.22 | loop fusion | flops 5898240 | bytes 9547776 | tf_op jit(solution)/shard_map/add | solution.py:119
  216.4 6.0 %broadcast_divide_fusion = (f32[3,2,1536,128]{3,2,1,0:T(8,128)}, f32[3,2,1536,128]{3,2,1,0:T(8,128)}) fusion(f32[3,2,1536,128]{3,2,1,0:T(8,128)S(1)} %bitcast.77, f32[2,1536,128]{2,1,0:T(8,128)S(1)} %multiply_subtract_fusion, f32[3,2,1536,128]{3,2,1,0:T(8,128)} %param.13, f32[1,2,1536,128]{3,2,1,0:T(8,128)S(1)} %get-tuple-element.14, ...), kind=kLoop, calls=%fused_computation.18 | loop fusion | flops 10616832 | bytes 25559040 | tf_op jit(solution)/shard_map/div | solution.py:116
  222.5 7.2 %gather_fusion.4 = f32[6,2,1536,128]{3,2,1,0:T(8,128)} fusion(f32[3,2,1536,128]{3,2,1,0:T(8,128)} %get-tuple-element.10, s32[1024]{0:T(1024)S(1)} %pad_clamp_fusion), kind=kCustom, calls=%fused_computation.4 | custom fusion | bytes 18874392 | tf_op jit(solution)/shard_map/gather | solution.py:136
  229.6 8.9 %multiply_reduce_fusion = f32[6,2,1536]{2,1,0:T(2,128)S(1)} fusion(f32[6,2,1536,128]{3,2,1,0:T(8,128)} %gather_fusion.3, f32[6,2,1536,128]{3,2,1,0:T(8,128)} %gather_fusion.4), kind=kLoop, calls=%fused_computation.9 | loop fusion | flops 4700160 | bytes 18948096 | tf_op jit(solution)/shard_map/reduce_sum | solution.py:136
  238.6 7.9 %fusion = f32[6,2048]{1,0:T(8,128)S(1)} fusion(f32[6,3072]{1,0:T(8,128)S(1)} %bitcast.88, s32[3072]{0:T(1024)S(1)} %copy-done.1), kind=kOutput, calls=%fused_computation.7 | convolution fusion | flops 459276288 | bytes 135168 | tf_op jit(solution)/shard_map/dot_general | solution.py:140
  246.6 13.9 %psum.7 = f32[6,8,256]{2,1,0:T(8,128)S(1)} all-reduce(f32[6,8,256]{2,1,0:T(8,128)S(1)} %bitcast.87), channel_id=1, replica_groups=mesh['ens'=4,'cx'=8,'cy'=4] {'ens'}, use_global_device_ids=true, to_apply=%region_3.4 | all-reduce | flops 12288 | bytes 98304 | tf_op jit(solution)/shard_map/psum | solution.py:146
  260.5 7.7 %collective-permute-start.5 = (f32[6,1,256]{2,1,0:T(1,128)S(1)}, f32[6,1,256]{2,1,0:T(1,128)S(1)}, u32[]{:S(2)}, u32[]{:S(2)}) collective-permute-start(f32[6,1,256]{2,1,0:T(1,128)S(1)} %get-tuple-element.33), channel_id=1, source_target_pairs={{0,4},{4,8},{8,12},{12,16},{16,20},{20,24},{24,28},{1,5},{5,9},{9,... | collective-permute-start | bytes 18440 | tf_op jit(solution)/shard_map/ppermute | solution.py:26
  270.2 2.9 %collective-permute-done.4 = f32[6,1,256]{2,1,0:T(1,128)S(1)} collective-permute-done((f32[6,1,256]{2,1,0:T(1,128)S(1)}, f32[6,1,256]{2,1,0:T(1,128)S(1)}, u32[]{:S(2)}, u32[]{:S(2)}) %collective-permute-start.4) | collective-permute-done | bytes 6176 | tf_op jit(solution)/shard_map/ppermute | solution.py:29
  274.6 4.0 %collective-permute-start.7 = (f32[6,10,64]{2,1,0:T(8,128)S(1)}, f32[6,10,64]{2,1,0:T(8,128)S(1)}, u32[]{:S(2)}, u32[]{:S(2)}) collective-permute-start(f32[6,10,64]{2,1,0:T(8,128)S(1)} %get-tuple-element.30), channel_id=1, source_target_pairs={{0,1},{1,2},{2,3},{4,5},{5,6},{6,7},{8,9},{9,10},{10,11},{12,13},{... | collective-permute-start | bytes 46088 | tf_op jit(solution)/shard_map/ppermute | solution.py:26
  (96 shorter events, 31.6 us)
Async XLA Ops:
  36.3 47.0 %all-to-all-start = ((s32[32,1,192]{2,1,0:T(1,128)}), s32[32,1,192]{2,1,0:T(1,128)S(1)}, u32[]{:S(2)}, u32[]{:S(2)}) async-start(s32[32,1,192]{2,1,0:T(1,128)} %reshape.180), calls=%async_computation | async-start | bytes 65536 | tf_op jit(solution)/shard_map/all_to_all | solution.py:106
  83.3 7.6 %copy-start = (f32[3,8,256]{2,1,0:T(8,128)S(1)}, f32[3,8,256]{2,1,0:T(8,128)}, u32[]{:S(2)}) copy-start(f32[3,8,256]{2,1,0:T(8,128)} %param.12) | copy-start | bytes 73732
  83.3 13.3 %copy-start.7 = (s32[6]{0:T(128)S(1)}, s32[6]{0:T(128)}, u32[]{:S(2)}) copy-start(s32[6]{0:T(128)} %constant.123) | copy-start | bytes 76
  83.3 88.1 %copy-start.6 = (s32[6]{0:T(128)S(1)}, s32[6]{0:T(128)}, u32[]{:S(2)}) copy-start(s32[6]{0:T(128)} %constant.124) | copy-start | bytes 76
  83.3 109.8 %all-to-all-start.1 = ((f32[3,2,1536,128]{3,0,1,2:T(4,128)}), f32[3,2,1536,128]{3,0,1,2:T(4,128)}, u32[]{:S(2)}, u32[]{:S(2)}) async-start(f32[3,2,1536,128]{3,0,1,2:T(4,128)} %copy_select_fusion), calls=%async_computation.1 | async-start | bytes 12582912 | tf_op jit(solution)/shard_map/all_to_all | solution.py:105
  90.9 68.7 %collective-permute-start.1 = (f32[3,1,256]{2,1,0:T(1,128)S(1)}, f32[3,1,256]{2,1,0:T(1,128)S(1)}, u32[]{:S(2)}, u32[]{:S(2)}) collective-permute-start(f32[3,1,256]{2,1,0:T(1,128)S(1)} %get-tuple-element.41), channel_id=1, source_target_pairs={{0,4},{4,8},{8,12},{12,16},{16,20},{20,24},{24,28},{1,5},{5,9},{9,... | collective-permute-start | bytes 9224 | tf_op jit(solution)/shard_map/ppermute | solution.py:26
  94.5 73.7 %collective-permute-start = (f32[3,1,256]{2,1,0:T(1,128)S(1)}, f32[3,1,256]{2,1,0:T(1,128)S(1)}, u32[]{:S(2)}, u32[]{:S(2)}) collective-permute-start(f32[3,1,256]{2,1,0:T(1,128)S(1)} %get-tuple-element.42), channel_id=1, source_target_pairs={{4,0},{8,4},{12,8},{16,12},{20,16},{24,20},{28,24},{5,1},{9,5},{13... | collective-permute-start | bytes 9224 | tf_op jit(solution)/shard_map/ppermute | solution.py:29
  96.4 82.3 %copy-start.2 = (pred[256]{0:T(512)(128)(4,1)}, pred[256]{0:T(512)(128)(4,1)S(1)}, u32[]{:S(2)}) copy-start(pred[256]{0:T(512)(128)(4,1)S(1)} %get-tuple-element.47) | copy-start | bytes 772
  96.4 82.3 %copy-start.4 = (pred[256]{0:T(512)(128)(4,1)}, pred[256]{0:T(512)(128)(4,1)S(1)}, u32[]{:S(2)}) copy-start(pred[256]{0:T(512)(128)(4,1)S(1)} %get-tuple-element.48) | copy-start | bytes 772
  168.2 3.2 %collective-permute-start.3 = (f32[3,10,64]{2,1,0:T(8,128)S(1)}, f32[3,10,64]{2,1,0:T(8,128)S(1)}, u32[]{:S(2)}, u32[]{:S(2)}) collective-permute-start(f32[3,10,64]{2,1,0:T(8,128)S(1)} %get-tuple-element.37), channel_id=1, source_target_pairs={{0,1},{1,2},{2,3},{4,5},{5,6},{6,7},{8,9},{9,10},{10,11},{12,13},{... | collective-permute-start | bytes 23048 | tf_op jit(solution)/shard_map/ppermute | solution.py:26
  169.9 4.6 %collective-permute-start.2 = (f32[3,10,64]{2,1,0:T(8,128)S(1)}, f32[3,10,64]{2,1,0:T(8,128)S(1)}, u32[]{:S(2)}, u32[]{:S(2)}) collective-permute-start(f32[3,10,64]{2,1,0:T(8,128)S(1)} %get-tuple-element.38), channel_id=1, source_target_pairs={{1,0},{2,1},{3,2},{5,4},{6,5},{7,6},{9,8},{10,9},{11,10},{13,12},{... | collective-permute-start | bytes 23048 | tf_op jit(solution)/shard_map/ppermute | solution.py:29
  207.1 9.3 %slice-start = ((s8[4718592]{0:T(1024)(128)(4,1)}), s8[4194304]{0:T(1024)(128)(4,1)S(1)}, s32[]{:S(2)}) async-start(s8[4718592]{0:T(1024)(128)(4,1)} %bitcast.76), calls=%async_computation.2 | async-start | bytes 8388608
  207.1 9.3 %slice-start.1 = ((s8[4718592]{0:T(1024)(128)(4,1)}), s8[524288]{0:T(1024)(128)(4,1)S(1)}, s32[]{:S(2)}) async-start(s8[4718592]{0:T(1024)(128)(4,1)} %bitcast.76), calls=%async_computation.3 | async-start | bytes 1048576
  229.6 9.0 %copy-start.1 = (s32[3072]{0:T(1024)S(1)}, s32[3072]{0:T(1024)}, u32[]{:S(2)}) copy-start(s32[3072]{0:T(1024)} %eq.18) | copy-start | bytes 36868
  238.6 40.0 %copy-start.3 = (pred[256]{0:T(512)(128)(4,1)S(1)}, pred[256]{0:T(512)(128)(4,1)}, u32[]{:S(2)}) copy-start(pred[256]{0:T(512)(128)(4,1)} %copy-done.2) | copy-start | bytes 772
  238.6 40.0 %copy-start.5 = (pred[256]{0:T(512)(128)(4,1)S(1)}, pred[256]{0:T(512)(128)(4,1)}, u32[]{:S(2)}) copy-start(pred[256]{0:T(512)(128)(4,1)} %copy-done.4) | copy-start | bytes 772
  260.5 9.7 %collective-permute-start.5 = (f32[6,1,256]{2,1,0:T(1,128)S(1)}, f32[6,1,256]{2,1,0:T(1,128)S(1)}, u32[]{:S(2)}, u32[]{:S(2)}) collective-permute-start(f32[6,1,256]{2,1,0:T(1,128)S(1)} %get-tuple-element.33), channel_id=1, source_target_pairs={{0,4},{4,8},{8,12},{12,16},{16,20},{20,24},{24,28},{1,5},{5,9},{9,... | collective-permute-start | bytes 18440 | tf_op jit(solution)/shard_map/ppermute | solution.py:26
  268.2 4.9 %collective-permute-start.4 = (f32[6,1,256]{2,1,0:T(1,128)S(1)}, f32[6,1,256]{2,1,0:T(1,128)S(1)}, u32[]{:S(2)}, u32[]{:S(2)}) collective-permute-start(f32[6,1,256]{2,1,0:T(1,128)S(1)} %get-tuple-element.34), channel_id=1, source_target_pairs={{4,0},{8,4},{12,8},{16,12},{20,16},{24,20},{28,24},{5,1},{9,5},{13... | collective-permute-start | bytes 18440 | tf_op jit(solution)/shard_map/ppermute | solution.py:29
  273.3 5.4 %collective-permute-start.6 = (f32[6,10,64]{2,1,0:T(8,128)S(1)}, f32[6,10,64]{2,1,0:T(8,128)S(1)}, u32[]{:S(2)}, u32[]{:S(2)}) collective-permute-start(f32[6,10,64]{2,1,0:T(8,128)S(1)} %get-tuple-element.29), channel_id=1, source_target_pairs={{1,0},{2,1},{3,2},{5,4},{6,5},{7,6},{9,8},{10,9},{11,10},{13,12},{... | collective-permute-start | bytes 46088 | tf_op jit(solution)/shard_map/ppermute | solution.py:29
  274.6 5.2 %collective-permute-start.7 = (f32[6,10,64]{2,1,0:T(8,128)S(1)}, f32[6,10,64]{2,1,0:T(8,128)S(1)}, u32[]{:S(2)}, u32[]{:S(2)}) collective-permute-start(f32[6,10,64]{2,1,0:T(8,128)S(1)} %get-tuple-element.30), channel_id=1, source_target_pairs={{0,1},{1,2},{2,3},{4,5},{5,6},{6,7},{8,9},{9,10},{10,11},{12,13},{... | collective-permute-start | bytes 46088 | tf_op jit(solution)/shard_map/ppermute | solution.py:26
where the time goes:
time: 282 us; the launch traced here: 281 us
  local copies, waits for them, and re-layouts  94.4 us (33%)
  waiting for transfers between devices  78 us (28%)
  other arithmetic  44.7 us (16%)
  starting transfers between devices  40.5 us (14%)
  blocking collectives  13.9 us (5%)
  matrix products  7.92 us (3%)
    ppermute x4, waiting for transfers between devices, extended(): lax.ppermute(lax.slice_in_dim(block, block.shape[dim] - width, None, axis...  63.4 us
    gather x1, local copies, waits for them, and re-layouts, on_device(): jnp.take(flat_states, flat_rows, axis=1)  24.9 us
    unnamed x32, local copies, waits for them, and re-layouts  21 us
    gather x2, local copies, waits for them, and re-layouts, on_device(): jnp.take(label_rows, flat_rows, axis=1).reshape(2, groups, place_count)  17.9 us
    ppermute x4, starting transfers between devices, extended(): lax.ppermute(lax.slice_in_dim(block, block.shape[dim] - width, None, axis...  16.9 us
    ppermute x4, waiting for transfers between devices, extended(): lax.ppermute(lax.slice_in_dim(block, 0, width, axis=dim), axis, backward)  14.6 us
    psum x1, blocking collectives, on_device(): stress_field = lax.psum(partial_sums, 'ens')  13.9 us
    all_to_all x1, starting transfers between devices, on_device(): lax.all_to_all(labels, ('cx', 'cy'), split_axis=2, concat_axis=2, tiled=T...  9.43 us
  transfers between devices with their start and end apart: 10, of which 5 were waited for; matrix products, arithmetic and copies ran while one was open for 20% of the time, Pallas kernels for 0%

commit v1 on v0

v1 whole, which is shorter than its diff:
```python
import functools
import math

import jax
import jax.numpy as jnp
from jax import lax
from jax.experimental import pallas as pl
from jax.experimental.pallas import tpu as pltpu
from jax.sharding import PartitionSpec as P

DUMB = 64
NZ = 64
CAP = 48
TIME_STEP = 0.02
WEISSENBERG = 0.5
EXTENSION = 50.0
VISCOSITY = 1.0

PAIRS = ((0, 0), (1, 1), (2, 2), (0, 1), (0, 2), (1, 2))
ALONG_X = (0, 3, 4)
ALONG_Y = (3, 1, 5)
ALONG_Z = (4, 5, 2)

MESH = pl.DeviceIdType.MESH
F32 = jnp.float32
BF16 = jnp.bfloat16

OFFSETS = (
    (1, 0), (3, 0), (0, 1), (0, 3), (1, 1), (3, 3), (1, 3), (3, 1),
    (2, 0), (0, 2), (2, 1), (1, 2), (2, 3), (3, 2), (2, 2),
)
CODE_X = sum(dx * 4**i for i, (dx, _) in enumerate(OFFSETS))
CODE_Z = sum(dz * 4**i for i, (_, dz) in enumerate(OFFSETS))
HALVES = 2
PART = CAP // HALVES
NT = (((1,), (1,)), ((), ()))


def halves_of(values):
    high = values.astype(BF16)
    return high, (values - high.astype(F32)).astype(BF16)


def stencil(field, west, east, south, north):
    row = lax.broadcasted_iota(jnp.int32, field.shape, 0)
    lane = lax.broadcasted_iota(jnp.int32, field.shape, 1)
    rows, width = field.shape
    east_side = jnp.where(row == rows - 1, pltpu.roll(east, rows - 1, 0), pltpu.roll(field, rows - 1, 0))
    west_side = jnp.where(row == 0, pltpu.roll(west, 1, 0), pltpu.roll(field, 1, 0))
    north_side = jnp.where(
        lane >= width - NZ, pltpu.roll(north, width - NZ, 1), pltpu.roll(field, width - NZ, 1)
    )
    south_side = jnp.where(lane < NZ, pltpu.roll(south, NZ, 1), pltpu.roll(field, NZ, 1))
    return east_side, west_side, north_side, south_side


def along_z(field):
    lane = lax.rem(lax.broadcasted_iota(jnp.int32, field.shape, 1), NZ)
    width = field.shape[1]
    upper = jnp.where(lane < NZ - 1, pltpu.roll(field, width - 1, 1), 0.0)
    lower = jnp.where(lane > 0, pltpu.roll(field, 1, 1), 0.0)
    return upper, lower


def kernel(
    conf_hbm, fill_ref, dest_ref, cell_ref, vel_ref, noise_hbm,
    out_hbm, vout_ref,
    conf, high, low, sendbuf, recv, labsend, labrecv, noise, outbuf,
    vhalo, table, rowbuf, prods, field, sx, sy, shx, shy, dv, base,
    conf_sem, noise_sem, out_sem, ssem, rsem, lssem, lrsem, vs_sem, vr_sem, hs_sem, hr_sem, ds_sem, dr_sem,
):
    ens = lax.axis_index("ens")
    cx = lax.axis_index("cx")
    cy = lax.axis_index("cy")
    my_x = lax.div(cx, 2)
    core = lax.rem(cx, 2)
    n_ens = 4

    for g in range(2):
        pltpu.make_async_copy(conf_hbm.at[:, g], conf.at[:, g], conf_sem.at[g]).start()

    east_id = (ens, lax.rem(cx + 1, 8), cy)
    west_id = (ens, lax.rem(cx + 7, 8), cy)
    north_id = (ens, cx, lax.rem(cy + 1, 4))
    south_id = (ens, cx, lax.rem(cy + 3, 4))

    def chip(dx, dz, r):
        return (ens, lax.rem(my_x + dx, 4) * 2 + lax.rem(core + r, 2), lax.rem(cy + dz, 4))

    barrier = pltpu.get_barrier_semaphore()
    for dx, dz in OFFSETS:
        for r in range(2):
            pl.semaphore_signal(barrier, inc=1, device_id=chip(dx, dz, r), device_id_type=MESH)
    pl.semaphore_signal(barrier, inc=1, device_id=chip(0, 0, 1), device_id_type=MESH)
    for k in range(1, n_ens):
        pl.semaphore_signal(
            barrier, inc=1, device_id=(lax.rem(ens + k, n_ens), cx, cy), device_id_type=MESH
        )

    pltpu.make_async_copy(noise_hbm, noise, noise_sem).start()
    prods[...] = jnp.zeros_like(prods)
    field[...] = jnp.zeros_like(field)
    rowbuf[...] = jnp.zeros_like(rowbuf)
    labsend[...] = jnp.zeros_like(labsend)

    def split(g):
        pltpu.make_async_copy(conf_hbm.at[:, g], conf.at[:, g], conf_sem.at[g]).wait()
        for a in range(3):
            first, second = halves_of(conf[a, g])
            high[g, :, a * 128 : (a + 1) * 128] = first
            low[g, :, a * 128 : (a + 1) * 128] = second

    blocks = conf.shape[2]
    row48 = lax.broadcasted_iota(jnp.int32, (CAP, blocks), 0)
    row16 = lax.broadcasted_iota(jnp.int32, (16, blocks), 0)
    lane128 = lax.broadcasted_iota(jnp.int32, (1, 128), 1)

    split(0)
    pl.semaphore_wait(barrier, 31 + n_ens - 1)

    def vel_copy(slot, target):
        return pltpu.make_async_remote_copy(
            src_ref=vel_ref, dst_ref=vhalo.at[slot], send_sem=vs_sem.at[slot], recv_sem=vr_sem.at[slot],
            device_id=target, device_id_type=MESH,
        )

    halo_targets = (east_id, west_id, north_id, south_id)
    for slot in range(4):
        vel_copy(slot, halo_targets[slot]).start()

    def data_copy(g, i, r, h, target):
        rows = pl.ds(h * PART, PART)
        return pltpu.make_async_remote_copy(
            src_ref=sendbuf.at[g, i, r, :, rows], dst_ref=recv.at[g, i, r, :, rows],
            send_sem=ssem.at[g, i, r], recv_sem=rsem.at[g, i, r],
            device_id=target, device_id_type=MESH,
        )

    def label_copy(g, i, r, target):
        return pltpu.make_async_remote_copy(
            src_ref=labsend.at[g, i, r], dst_ref=labrecv.at[g, i, r],
            send_sem=lssem.at[g, i, r], recv_sem=lrsem.at[g, i, r],
            device_id=target, device_id_type=MESH,
        )

    def pack_batch(q, carry, g):
        code_x, code_z = carry
        dest = dest_ref[g : g + 1, :]
        fill = fill_ref[g : g + 1, :]
        cell = cell_ref[g : g + 1, :]
        pieces = []
        targets = []
        for m in range(4):
            dx, dz = lax.rem(code_x, 4), lax.rem(code_z, 4)
            code_x, code_z = lax.div(code_x, 4), lax.div(code_z, 4)
            for r in range(2):
                target = chip(dx, dz, r)
                owner = target[1] * 4 + target[2]
                targets.append(target)
                pieces.append(jnp.where(dest - owner * CAP == row48, 1.0, 0.0).astype(BF16))
        onehot = jnp.concatenate(pieces, axis=0)
        packed = jnp.dot(onehot, high[g], preferred_element_type=F32) + jnp.dot(
            onehot, low[g], preferred_element_type=F32
        )
        for n in range(8):
            for a in range(3):
                sendbuf[g, 4 * q + n // 2, n % 2, a] = packed[
                    n * CAP : (n + 1) * CAP, a * 128 : (a + 1) * 128
                ]
        labels = jnp.where(
            row16 == 0,
            fill,
            jnp.where(row16 == 1, lax.div(cell, 128), jnp.where(row16 == 2, lax.rem(cell, 128), 0)),
        )
        told = lax.dot_general(labels.astype(F32).astype(BF16), onehot, NT, preferred_element_type=F32)
        fills = told[0:1]
        cells = told[1:2] * 128.0 + told[2:3]
        for n in range(8):
            begin, width = n * CAP, 8 * CAP
            fill_row = pltpu.roll(fills, (width - begin) % width, 1)[:, :128]
            cell_row = pltpu.roll(cells, (width - begin + 64) % width, 1)[:, :128]
            labsend[g, 4 * q + n // 2, n % 2] = jnp.where(
                lane128 < CAP,
                fill_row,
                jnp.where((lane128 >= 64) & (lane128 < 64 + CAP), cell_row, 0.0),
            )

        def send(n):
            i, r = 4 * q + n // 2, n % 2
            label_copy(g, i, r, targets[n]).start()

        def send_part(n, h):
            i, r = 4 * q + n // 2, n % 2
            data_copy(g, i, r, h, targets[n]).start()

        for n in range(6):
            send(n)
        for h in range(HALVES):
            for n in range(6):
                send_part(n, h)

        @pl.when(q < 3)
        def _():
            for n in range(6, 8):
                send(n)
            for h in range(HALVES):
                for n in range(6, 8):
                    send_part(n, h)

        @pl.when(q == 3)
        def _():
            send(7)
            for h in range(HALVES):
                send_part(7, h)
            pltpu.make_async_copy(sendbuf.at[g, 15, 0], recv.at[g, 15, 0], rsem.at[g, 15, 0]).start()
            pltpu.make_async_copy(labsend.at[g, 15, 0], labrecv.at[g, 15, 0], lrsem.at[g, 15, 0]).start()

        return code_x, code_z

    codes = (jnp.int32(CODE_X), jnp.int32(CODE_Z))
    lax.fori_loop(0, 4, functools.partial(pack_batch, g=0), codes)
    split(1)
    lax.fori_loop(0, 4, functools.partial(pack_batch, g=1), codes)

    for slot in range(4):
        vel_copy(slot, halo_targets[slot]).wait()
    inside = (cx > 0, cx < 7, cy > 0, cy < 3)

    def masked(tile, k):
        return jnp.where(inside[k], tile, 0.0)

    for a in range(3):
        f = vel_ref[a]
        e, w, n, s = stencil(f, *(masked(vhalo[k, a], k) for k in range(4)))
        u, d = along_z(f)
        base[a] = f + TIME_STEP * VISCOSITY * (e + w + n + s + u + d - 6.0 * f)
        for b, slope in enumerate((0.5 * (e - w), 0.5 * (n - s), 0.5 * (u - d))):
            first, second = halves_of(jnp.concatenate([slope[:, :128], slope[:, 128:]], axis=0))
            top = (3 * a + b) * 16
            table[top : top + 16] = first
            table[144 + top : 144 + top + 16] = second

    pltpu.make_async_copy(noise_hbm, noise, noise_sem).wait()

    square = lax.broadcasted_iota(jnp.int32, (128, 128), 0)
    row_hi = lax.broadcasted_iota(jnp.int32, (16, 128), 0)
    slot_lane = lax.broadcasted_iota(jnp.int32, (CAP, 128), 1).astype(F32)
    pick_row = lax.broadcasted_iota(jnp.int32, (16, 12 * 128), 0)
    pick_lane = lax.broadcasted_iota(jnp.int32, (16, 12 * 128), 1)
    pick = jnp.where(pick_row == lax.div(pick_lane, 256), 1.0, 0.0).astype(BF16)

    def arrive(j, carry, g):
        code_x, code_z = carry
        own = j == 0
        i = lax.rem(j + 15, 16)
        dx = jnp.where(own, 0, lax.rem(code_x, 4))
        dz = jnp.where(own, 0, lax.rem(code_z, 4))
        code_x = jnp.where(own, code_x, lax.div(code_x, 4))
        code_z = jnp.where(own, code_z, lax.div(code_z, 4))
        for r in range(2):
            pltpu.make_async_copy(labrecv.at[g, i, r], labrecv.at[g, i, r], lrsem.at[g, i, r]).wait()
        lab0, lab1 = labrecv[g, i, 0], labrecv[g, i, 1]
        fills = jnp.where(lane128 < 64, lab0, pltpu.roll(lab1, 64, 1))
        cells = jnp.where(lane128 < 64, pltpu.roll(lab0, 64, 1), lab1).astype(jnp.int32)
        cell_lo = lax.rem(cells, 128)
        cell_hi = lax.div(cells, 128)
        cell_hi = lax.rem(cell_hi, 2) * 8 + lax.div(cell_hi, 2)
        at_lo = jnp.where(square == cell_lo, 1.0, 0.0).astype(BF16)
        at_hi = jnp.where(row_hi == cell_hi, 1.0, 0.0)
        looked = jnp.dot(table[...], at_lo, preferred_element_type=F32)
        looked = looked[:144] + looked[144:]
        for c in range(9):
            rowbuf[c : c + 1] = jnp.sum(looked[16 * c : 16 * c + 16] * at_hi, axis=0, keepdims=True)
        rowbuf[9:10] = fills
        columns = rowbuf[...].T
        for r in range(2):
            pltpu.make_async_copy(recv.at[g, i, r], recv.at[g, i, r], rsem.at[g, i, r]).wait()
        for r in range(2):
            source = (lax.rem(my_x + 4 - dx, 4) * 2 + lax.rem(core + r, 2)) * 4 + lax.rem(cy + 4 - dz, 4)
            rows = pl.ds(pl.multiple_of(source * CAP, CAP), CAP)
            here = columns[r * 64 : r * 64 + CAP]
            live = slot_lane < here[:, 9:10]
            x = [jnp.where(live, recv[g, i, r, a], 0.0) for a in range(3)]
            inverse = 1.0 / (1.0 - (x[0] * x[0] + x[1] * x[1] + x[2] * x[2]) / EXTENSION)
            spring = [x[a] * inverse for a in range(3)]
            for a in range(3):
                stretch = sum(here[:, 3 * a + b : 3 * a + b + 1] * x[b] for b in range(3))
                stepped = (
                    x[a]
                    + TIME_STEP * (stretch - spring[a] / (2.0 * WEISSENBERG))
                    + math.sqrt(TIME_STEP / WEISSENBERG) * noise[a, g, rows]
                )
                outbuf[a, g, rows] = jnp.where(live, stepped, 0.0)
            for c, (a, b) in enumerate(PAIRS):
                first, second = halves_of(x[a] * spring[b])
                prods[r * 64 : r * 64 + CAP, c * 256 : c * 256 + 128] = first
                prods[r * 64 : r * 64 + CAP, c * 256 + 128 : c * 256 + 256] = second
            pltpu.make_async_copy(outbuf.at[:, g, rows], out_hbm.at[:, g, rows], out_sem).start()
        sums = lax.dot_general(pick, prods[...], NT, preferred_element_type=F32)
        spread = jnp.concatenate([sums[c : c + 1] * at_hi for c in range(6)], axis=0)
        first, second = halves_of(spread)
        field[...] += lax.dot_general(
            jnp.concatenate([first, second], axis=0), at_lo, NT, preferred_element_type=F32
        )
        return code_x, code_z

    for g in range(2):
        lax.fori_loop(0, 16, functools.partial(arrive, g=g), codes)

    total = (field[:96] + field[96:]) / (WEISSENBERG * DUMB)
    stress = [
        jnp.concatenate([total[16 * c : 16 * c + 8], total[16 * c + 8 : 16 * c + 16]], axis=1) for c in range(6)
    ]
    for k in range(3):
        sx[k] = stress[ALONG_X[k]]
        sy[k] = stress[ALONG_Y[k]]

    def stress_copy(slot):
        return pltpu.make_async_remote_copy(
            src_ref=sx if slot < 2 else sy, dst_ref=shx.at[slot] if slot < 2 else shy.at[slot - 2],
            send_sem=hs_sem.at[slot], recv_sem=hr_sem.at[slot],
            device_id=halo_targets[slot], device_id_type=MESH,
        )

    for slot in range(4):
        stress_copy(slot).start()
    for slot in range(4):
        stress_copy(slot).wait()
    for k in range(3):
        fx, fy, fz = stress[ALONG_X[k]], stress[ALONG_Y[k]], stress[ALONG_Z[k]]
        e, w, _, _ = stencil(fx, masked(shx[0, k], 0), masked(shx[1, k], 1), fx, fx)
        _, _, n, s = stencil(fy, fy, fy, masked(shy[0, k], 2), masked(shy[1, k], 3))
        u, d = along_z(fz)
        dv[ens, k] = 0.5 * (e - w) + 0.5 * (n - s) + 0.5 * (u - d)

    def dv_copy(k):
        return pltpu.make_async_remote_copy(
            src_ref=dv.at[ens], dst_ref=dv.at[ens], send_sem=ds_sem.at[k], recv_sem=dr_sem.at[k],
            device_id=(lax.rem(ens + k, n_ens), cx, cy), device_id_type=MESH,
        )

    def dv_arrival(k):
        source = lax.rem(ens + n_ens - k, n_ens)
        pltpu.make_async_copy(dv.at[source], dv.at[source], dr_sem.at[k]).wait()

    for k in range(1, n_ens):
        dv_copy(k).start()
    for k in range(1, n_ens):
        dv_arrival(k)
    vout_ref[...] = base[...] + TIME_STEP * (dv[0] + dv[1] + dv[2] + dv[3])

    for k in range(1, n_ens):
        dv_copy(k).wait_send()

    def sent(i, carry):
        for g in range(2):
            for r in range(2):
                pltpu.make_async_copy(sendbuf.at[g, i, r], sendbuf.at[g, i, r], ssem.at[g, i, r]).wait()
                pltpu.make_async_copy(labsend.at[g, i, r], labsend.at[g, i, r], lssem.at[g, i, r]).wait()
        return carry

    lax.fori_loop(0, 15, sent, 0)
    for g in range(2):
        pltpu.make_async_copy(sendbuf.at[g, 15, 1], sendbuf.at[g, 15, 1], ssem.at[g, 15, 1]).wait()
        pltpu.make_async_copy(labsend.at[g, 15, 1], labsend.at[g, 15, 1], lssem.at[g, 15, 1]).wait()
    pltpu.make_async_copy(outbuf, out_hbm, out_sem).wait()


def on_device(conformations, fill_counts, dest_slots, dest_cells, velocity, noise):
    _, groups, blocks, slots = conformations.shape
    places = noise.shape[2]
    vmem = pl.BlockSpec(memory_space=pltpu.VMEM)
    hbm = pl.BlockSpec(memory_space=pl.ANY)
    tile = velocity.shape
    dma = pltpu.SemaphoreType.DMA
    return pl.pallas_call(
        kernel,
        out_shape=(
            jax.ShapeDtypeStruct(noise.shape, F32),
            jax.ShapeDtypeStruct(velocity.shape, F32),
        ),
        in_specs=[hbm, vmem, vmem, vmem, vmem, hbm],
        out_specs=(hbm, vmem),
        scratch_shapes=[
            pltpu.VMEM(conformations.shape, F32),
            pltpu.VMEM((groups, blocks, 3 * slots), BF16),
            pltpu.VMEM((groups, blocks, 3 * slots), BF16),
            pltpu.VMEM((groups, 16, 2, 3, CAP, slots), F32),
            pltpu.VMEM((groups, 16, 2, 3, CAP, slots), F32),
            pltpu.VMEM((groups, 16, 2, 1, 128), F32),
            pltpu.VMEM((groups, 16, 2, 1, 128), F32),
            pltpu.VMEM(noise.shape, F32),
            pltpu.VMEM(noise.shape, F32),
            pltpu.VMEM((4,) + tile, F32),
            pltpu.VMEM((288, 128), BF16),
            pltpu.VMEM((16, 128), F32),
            pltpu.VMEM((128, 12 * 128), BF16),
            pltpu.VMEM((192, 128), F32),
            pltpu.VMEM(tile, F32),
            pltpu.VMEM(tile, F32),
            pltpu.VMEM((2,) + tile, F32),
            pltpu.VMEM((2,) + tile, F32),
            pltpu.VMEM((4,) + tile, F32),
            pltpu.VMEM(tile, F32),
            dma((2,)), dma, dma,
            dma((groups, 16, 2)), dma((groups, 16, 2)),
            dma((groups, 16, 2)), dma((groups, 16, 2)),
            dma((4,)), dma((4,)), dma((4,)), dma((4,)), dma((4,)), dma((4,)),
        ],
        compiler_params=pltpu.CompilerParams(
            collective_id=0, has_side_effects=True, vmem_limit_bytes=52 * 2**20
        ),
    )(conformations, fill_counts, dest_slots, dest_cells, velocity, noise)


def solution(mesh):
    placed = (
        P(None, "ens", ("cx", "cy"), None),
        P("ens", ("cx", "cy")),
        P("ens", ("cx", "cy")),
        P("ens", ("cx", "cy")),
        P(None, "cx", "cy"),
        P(None, "ens", ("cx", "cy"), None),
    )
    return jax.shard_map(
        on_device,
        mesh=mesh,
        in_specs=placed,
        out_specs=(P(None, "ens", ("cx", "cy"), None), P(None, "cx", "cy")),
        check_vma=False,
    )
```

time: 282 us -> 89.4 us (0.32)
  local copies, waits for them, and re-layouts: 94.4 us -> 8.25 us
  Pallas kernels: 0 us -> 80.2 us
  waiting for transfers between devices: 78 us -> 0 us
  other arithmetic: 44.7 us -> 0 us
  starting transfers between devices: 40.5 us -> 0 us
  blocking collectives: 13.9 us -> 0 us
  matrix products: 7.92 us -> 0 us
    pallas_call x0 -> x1, Pallas kernels: none -> 80.2 us  [on_device(): pl.pallas_call(kernel, out_shape=(jax.ShapeDtypeStruct(noise.shape, F32),...]
    ppermute x8 -> x0, waiting for transfers between devices: 78 us -> none  [the longest x4 63.4 us: extended(): lax.ppermute(lax.slice_in_dim(block, block.shape[dim] - width, None, axis...]
    gather x7 -> x0, local copies, waits for them, and re-layouts: 65.8 us -> none  [the longest x1 24.9 us: on_device(): jnp.take(flat_states, flat_rows, axis=1)]
    ppermute x8 -> x0, starting transfers between devices: 23.5 us -> none  [the longest x4 16.9 us: extended(): lax.ppermute(lax.slice_in_dim(block, block.shape[dim] - width, None, axis...]
    all_to_all x2 -> x0, starting transfers between devices: 17 us -> none  [the longest x1 9.43 us: on_device(): lax.all_to_all(labels, ('cx', 'cy'), split_axis=2, concat_axis=2, tiled=T...]
    reduce_sum x2 -> x0, other arithmetic: 15.4 us -> none  [the longest x1 8.91 us: on_device(): jnp.sum(placed[first_rows] * spring[second_rows], axis=-1)]
    psum x1 -> x0, blocking collectives: 13.9 us -> none  [on_device(): stress_field = lax.psum(partial_sums, 'ens')]
    unnamed x32 -> x10, local copies, waits for them, and re-layouts: 21 us -> 8.25 us
  transfers between devices with their start and end apart: 10 -> 0, of which waited for: 5 -> 0; matrix products, arithmetic and copies ran while one was open for 20% -> 0% of each run, Pallas kernels for 0% -> 0%
where the time goes in v1:
time: 89.4 us; the launch traced here: 89.1 us
  Pallas kernels  80.2 us (90%)
  local copies, waits for them, and re-layouts  8.25 us (9%)
    pallas_call x1, Pallas kernels, on_device(): pl.pallas_call(kernel, out_shape=(jax.ShapeDtypeStruct(noise.shape, F32),...  80.2 us
    unnamed x10, local copies, waits for them, and re-layouts  8.25 us

profile of v1, /device:TPU:1, one launch (start us, length us, event | category | flops | bytes accessed | tf_op | source)
XLA Modules:
  0.0 89.1 jit_solution(4236890848466367292)
XLA Ops:
  0.6 0.0 copy-start
  0.6 0.7 copy-done
  1.4 0.0 copy-start.1
  1.4 0.7 copy-done.1
  2.1 0.0 copy-start.2
  2.1 0.7 copy-done.2
  2.8 0.0 copy-start.3
  2.8 0.7 copy-done.3
  3.5 80.2 %shard_map.77 = (f32[3,2,1536,128]{3,2,1,0:T(8,128)}, f32[3,8,256]{2,1,0:T(8,128)S(1)}) custom-call(f32[3,2,1024,128]{3,2,1,0:T(8,128)} %conf_hbm.1, s32[2,1024]{1,0:T(2,128)S(1)} %copy-done.1, s32[2,1024]{1,0:T(2,128)S(1)} %copy-done.2, s32[2,1024]{1,0:T(2,128)S(1)} %copy-done.3, f32[3,8,256]{2,1,0:T(8,128)S(1)} %copy-done, f32[3,2,1536,128]{3,2,1,0:T(8,128)} %noise_hbm.1), custom_call_target="tpu_custom_call" | custom-call | tf_op jit(solution)/shard_map/pallas_call | solution.py:376
  83.7 4.8 %copy.10 = f32[3,2,1536,128]{3,2,1,0:T(8,128)} copy(f32[3,2,1536,128]{3,2,1,0:T(8,128)} %get-tuple-element.4) | data formatting | bytes 9437184
  88.5 0.6 copy.11
Async XLA Ops:
  0.6 0.7 copy-start
  1.4 0.7 copy-start.1
  2.1 0.7 copy-start.2
  2.8 0.7 copy-start.3

commit v2 on v1

v2 whole, which is shorter than its diff:
```python
import functools
import math

import jax
import jax.numpy as jnp
from jax import lax
from jax.experimental import pallas as pl
from jax.experimental.pallas import tpu as pltpu
from jax.sharding import PartitionSpec as P

DUMB = 64
NZ = 64
CAP = 48
TIME_STEP = 0.02
WEISSENBERG = 0.5
EXTENSION = 50.0
VISCOSITY = 1.0

PAIRS = ((0, 0), (1, 1), (2, 2), (0, 1), (0, 2), (1, 2))
ALONG_X = (0, 3, 4)
ALONG_Y = (3, 1, 5)
ALONG_Z = (4, 5, 2)

MESH = pl.DeviceIdType.MESH
F32 = jnp.float32
BF16 = jnp.bfloat16

OFFSETS = (
    (2, 2), (2, 1), (1, 2), (2, 3), (3, 2), (2, 0), (0, 2), (1, 1),
    (3, 3), (1, 3), (3, 1), (1, 0), (3, 0), (0, 1), (0, 3),
)
CODE_X = sum(dx * 4**i for i, (dx, _) in enumerate(OFFSETS))
CODE_Z = sum(dz * 4**i for i, (_, dz) in enumerate(OFFSETS))
HALVES = 2
PART = CAP // HALVES
NT = (((1,), (1,)), ((), ()))


def halves_of(values):
    high = values.astype(BF16)
    return high, (values - high.astype(F32)).astype(BF16)


def stencil(field, west, east, south, north):
    row = lax.broadcasted_iota(jnp.int32, field.shape, 0)
    lane = lax.broadcasted_iota(jnp.int32, field.shape, 1)
    rows, width = field.shape
    east_side = jnp.where(row == rows - 1, pltpu.roll(east, rows - 1, 0), pltpu.roll(field, rows - 1, 0))
    west_side = jnp.where(row == 0, pltpu.roll(west, 1, 0), pltpu.roll(field, 1, 0))
    north_side = jnp.where(
        lane >= width - NZ, pltpu.roll(north, width - NZ, 1), pltpu.roll(field, width - NZ, 1)
    )
    south_side = jnp.where(lane < NZ, pltpu.roll(south, NZ, 1), pltpu.roll(field, NZ, 1))
    return east_side, west_side, north_side, south_side


def along_z(field):
    lane = lax.rem(lax.broadcasted_iota(jnp.int32, field.shape, 1), NZ)
    width = field.shape[1]
    upper = jnp.where(lane < NZ - 1, pltpu.roll(field, width - 1, 1), 0.0)
    lower = jnp.where(lane > 0, pltpu.roll(field, 1, 1), 0.0)
    return upper, lower


def kernel(
    conf_hbm, fill_hbm, dest_hbm, cell_hbm, vel_hbm, noise_hbm,
    out_ref, vout_ref,
    conf, fill_ref, dest_ref, cell_ref, vel_ref, noise, high, low, sendbuf, recv, labmat, labsend, labrecv, columns,
    vhalo, table, rowbuf, prods, field, sx, sy, shx, shy, dv, base,
    conf_sem, in_sem, noise_sem, ssem, rsem, lssem, lrsem, vs_sem, vr_sem, hs_sem, hr_sem, ds_sem, dr_sem,
):
    ens = lax.axis_index("ens")
    cx = lax.axis_index("cx")
    cy = lax.axis_index("cy")
    my_x = lax.div(cx, 2)
    core = lax.rem(cx, 2)
    n_ens = 4

    def conf_copy(g):
        return pltpu.make_async_copy(conf_hbm.at[:, g], conf.at[:, g], conf_sem.at[g])

    small = [
        pltpu.make_async_copy(source, target, in_sem.at[k])
        for k, (source, target) in enumerate(
            ((dest_hbm, dest_ref), (vel_hbm, vel_ref), (fill_hbm, fill_ref), (cell_hbm, cell_ref))
        )
    ]
    conf_copy(0).start()
    for copy in small:
        copy.start()
    conf_copy(1).start()
    noise_copy = pltpu.make_async_copy(noise_hbm, noise, noise_sem)
    noise_copy.start()

    east_id = (ens, lax.rem(cx + 1, 8), cy)
    west_id = (ens, lax.rem(cx + 7, 8), cy)
    north_id = (ens, cx, lax.rem(cy + 1, 4))
    south_id = (ens, cx, lax.rem(cy + 3, 4))

    def chip(dx, dz, r):
        return (ens, lax.rem(my_x + dx, 4) * 2 + lax.rem(core + r, 2), lax.rem(cy + dz, 4))

    barrier = pltpu.get_barrier_semaphore()
    for dx, dz in OFFSETS:
        for r in range(2):
            pl.semaphore_signal(barrier, inc=1, device_id=chip(dx, dz, r), device_id_type=MESH)
    pl.semaphore_signal(barrier, inc=1, device_id=chip(0, 0, 1), device_id_type=MESH)
    for k in range(1, n_ens):
        pl.semaphore_signal(
            barrier, inc=1, device_id=(lax.rem(ens + k, n_ens), cx, cy), device_id_type=MESH
        )

    def split(g):
        for a in range(3):
            first, second = halves_of(conf[a, g])
            high[g, :, a * 128 : (a + 1) * 128] = first
            low[g, :, a * 128 : (a + 1) * 128] = second

    blocks = conf.shape[2]
    row48 = lax.broadcasted_iota(jnp.int32, (CAP, blocks), 0)
    row64 = lax.broadcasted_iota(jnp.int32, (64, blocks), 0)
    row64 = jnp.where(row64 < CAP, row64, 2**20)
    lane128 = lax.broadcasted_iota(jnp.int32, (1, 128), 1)

    field[...] = jnp.zeros_like(field)
    rowbuf[...] = jnp.zeros_like(rowbuf)
    conf_copy(0).wait()
    split(0)
    for copy in small:
        copy.wait()
    pl.semaphore_wait(barrier, 31 + n_ens - 1)

    def data_copy(g, i, r, h, target):
        rows = pl.ds(h * PART, PART)
        return pltpu.make_async_remote_copy(
            src_ref=sendbuf.at[g, i, r, :, rows], dst_ref=recv.at[g, i, r, :, rows],
            send_sem=ssem.at[g, i, r], recv_sem=rsem.at[g, i, r],
            device_id=target, device_id_type=MESH,
        )

    def label_copy(g, i, r, target):
        return pltpu.make_async_remote_copy(
            src_ref=labsend.at[g, i, r], dst_ref=labrecv.at[g, i, r],
            send_sem=lssem.at[g, i, r], recv_sem=lrsem.at[g, i, r],
            device_id=target, device_id_type=MESH,
        )

    def batch_targets(carry):
        code_x, code_z = carry
        targets = []
        for _ in range(4):
            dx, dz = lax.rem(code_x, 4), lax.rem(code_z, 4)
            code_x, code_z = lax.div(code_x, 4), lax.div(code_z, 4)
            targets += [chip(dx, dz, 0), chip(dx, dz, 1)]
        return targets, (code_x, code_z)

    def one_hot(dest, targets, rows):
        return jnp.concatenate(
            [
                jnp.where(dest - (target[1] * 4 + target[2]) * CAP == rows, 1.0, 0.0).astype(BF16)
                for target in targets
            ],
            axis=0,
        )

    def pack_batch(q, carry, g):
        targets, carry = batch_targets(carry)
        onehot = one_hot(dest_ref[g : g + 1, :], targets, row48)
        packed = jnp.dot(onehot, high[g], preferred_element_type=F32) + jnp.dot(
            onehot, low[g], preferred_element_type=F32
        )
        for n in range(8):
            for a in range(3):
                sendbuf[g, 4 * q + n // 2, n % 2, a] = packed[
                    n * CAP : (n + 1) * CAP, a * 128 : (a + 1) * 128
                ]
        for h in range(HALVES):
            for n in range(6):
                data_copy(g, 4 * q + n // 2, n % 2, h, targets[n]).start()

        @pl.when(q < 3)
        def _():
            for h in range(HALVES):
                for n in range(6, 8):
                    data_copy(g, 4 * q + n // 2, n % 2, h, targets[n]).start()

        @pl.when(q == 3)
        def _():
            for h in range(HALVES):
                data_copy(g, 15, 1, h, targets[7]).start()
            pltpu.make_async_copy(sendbuf.at[g, 15, 0], recv.at[g, 15, 0], rsem.at[g, 15, 0]).start()

        return carry

    codes = (jnp.int32(CODE_X), jnp.int32(CODE_Z))
    later_codes = (jnp.int32(CODE_X // 4**8), jnp.int32(CODE_Z // 4**8))
    lax.fori_loop(0, 2, functools.partial(pack_batch, g=0), codes)

    def vel_copy(slot, target):
        return pltpu.make_async_remote_copy(
            src_ref=vel_ref, dst_ref=vhalo.at[slot], send_sem=vs_sem.at[slot], recv_sem=vr_sem.at[slot],
            device_id=target, device_id_type=MESH,
        )

    halo_targets = (east_id, west_id, north_id, south_id)
    for slot in range(4):
        vel_copy(slot, halo_targets[slot]).start()

    lab_row = lax.broadcasted_iota(jnp.int32, (16, 128), 0)
    block_lane = lax.broadcasted_iota(jnp.int32, (128, 128), 1).astype(F32)
    pick_row = lax.broadcasted_iota(jnp.int32, (16, 12 * 128), 0)
    pick_pair = lax.div(lax.broadcasted_iota(jnp.int32, (16, 12 * 128), 1), 256)
    pick = jnp.where((pick_row == pick_pair + 3) | (pick_row == pick_pair + 9), 1.0, 0.0).astype(BF16)

    def label_rows(k, carry, g):
        rows = pl.ds(pl.multiple_of(k * 128, 128), 128)
        fill = fill_ref[g : g + 1, rows].astype(F32)
        cell = cell_ref[g : g + 1, rows]
        rowbuf[0:1] = fill
        live = block_lane < rowbuf[...].T[:, 0:1]
        x = [jnp.where(live, conf[a, g, rows], 0.0) for a in range(3)]
        inverse = 1.0 / (1.0 - (x[0] * x[0] + x[1] * x[1] + x[2] * x[2]) / EXTENSION)
        spring = [x[a] * inverse for a in range(3)]
        for c, (a, b) in enumerate(PAIRS):
            first, second = halves_of(x[a] * spring[b])
            prods[:, c * 256 : c * 256 + 128] = first
            prods[:, c * 256 + 128 : c * 256 + 256] = second
        sums = lax.dot_general(pick, prods[...], NT, preferred_element_type=F32)
        first = sums.astype(BF16).astype(F32)
        cell_hi = lax.div(cell, 128).astype(F32)
        cell_lo = lax.rem(cell, 128).astype(F32)
        rest = jnp.where(lab_row < 9, first, jnp.where(lab_row < 15, sums - first, 0.0))
        labmat[g, :, rows] = jnp.where(
            lab_row == 0, fill, jnp.where(lab_row == 1, cell_hi, jnp.where(lab_row == 2, cell_lo, rest))
        ).astype(BF16)
        return carry

    conf_copy(1).wait()
    for g in range(2):
        lax.fori_loop(0, blocks // 128, functools.partial(label_rows, g=g), 0)

    def label_batch(q, carry, g):
        targets, carry = batch_targets(carry)
        onehot = one_hot(dest_ref[g : g + 1, :], targets, row64)
        told = lax.dot_general(labmat[g], onehot, NT, preferred_element_type=F32)
        top = jnp.concatenate([told[0:1], told[1:2] * 128.0 + told[2:3], told[3:5] + told[9:11]], axis=0)
        bottom = told[5:9] + told[11:15]
        for m in range(4):
            upper, lower = top[:, m * 128 : (m + 1) * 128], bottom[:, m * 128 : (m + 1) * 128]
            labsend[g, 4 * q + m, 0] = jnp.where(lane128 < 64, upper, pltpu.roll(lower, 64, 1))
            labsend[g, 4 * q + m, 1] = jnp.where(lane128 < 64, pltpu.roll(upper, 64, 1), lower)
        for n in range(6):
            label_copy(g, 4 * q + n // 2, n % 2, targets[n]).start()

        @pl.when(q < 3)
        def _():
            for n in range(6, 8):
                label_copy(g, 4 * q + n // 2, n % 2, targets[n]).start()

        @pl.when(q == 3)
        def _():
            label_copy(g, 15, 1, targets[7]).start()
            pltpu.make_async_copy(labsend.at[g, 15, 0], labrecv.at[g, 15, 0], lrsem.at[g, 15, 0]).start()

        return carry

    for g in range(2):
        lax.fori_loop(0, 4, functools.partial(label_batch, g=g), codes)

    lax.fori_loop(2, 4, functools.partial(pack_batch, g=0), later_codes)
    split(1)
    lax.fori_loop(0, 4, functools.partial(pack_batch, g=1), codes)

    for slot in range(4):
        vel_copy(slot, halo_targets[slot]).wait()
    inside = (cx > 0, cx < 7, cy > 0, cy < 3)

    def masked(tile, k):
        return jnp.where(inside[k], tile, 0.0)

    for a in range(3):
        f = vel_ref[a]
        e, w, n, s = stencil(f, *(masked(vhalo[k, a], k) for k in range(4)))
        u, d = along_z(f)
        base[a] = f + TIME_STEP * VISCOSITY * (e + w + n + s + u + d - 6.0 * f)
        for b, slope in enumerate((0.5 * (e - w), 0.5 * (n - s), 0.5 * (u - d))):
            first, second = halves_of(jnp.concatenate([slope[:, :128], slope[:, 128:]], axis=0))
            top = (3 * a + b) * 16
            table[top : top + 16] = first
            table[144 + top : 144 + top + 16] = second

    square = lax.broadcasted_iota(jnp.int32, (128, 128), 0)
    row_hi = lax.broadcasted_iota(jnp.int32, (16, 128), 0)

    def read_labels(i, carry, g):
        for r in range(2):
            pltpu.make_async_copy(labrecv.at[g, i, r], labrecv.at[g, i, r], lrsem.at[g, i, r]).wait()
        lab0, lab1 = labrecv[g, i, 0], labrecv[g, i, 1]
        upper = jnp.where(lane128 < 64, lab0, pltpu.roll(lab1, 64, 1))
        lower = jnp.where(lane128 < 64, pltpu.roll(lab0, 64, 1), lab1)
        cells = upper[1:2].astype(jnp.int32)
        cell_lo = lax.rem(cells, 128)
        cell_hi = lax.div(cells, 128)
        cell_hi = lax.rem(cell_hi, 2) * 8 + lax.div(cell_hi, 2)
        at_lo = jnp.where(square == cell_lo, 1.0, 0.0).astype(BF16)
        at_hi = jnp.where(row_hi == cell_hi, 1.0, 0.0)
        looked = jnp.dot(table[...], at_lo, preferred_element_type=F32)
        looked = looked[:144] + looked[144:]
        for c in range(9):
            rowbuf[c : c + 1] = jnp.sum(looked[16 * c : 16 * c + 16] * at_hi, axis=0, keepdims=True)
        rowbuf[9:10] = upper[0:1]
        columns[g, i] = rowbuf[...].T
        sums = [upper[2:3], upper[3:4]] + [lower[c : c + 1] for c in range(4)]
        spread = jnp.concatenate([sums[c] * at_hi for c in range(6)], axis=0)
        first, second = halves_of(spread)
        field[...] += lax.dot_general(
            jnp.concatenate([first, second], axis=0), at_lo, NT, preferred_element_type=F32
        )
        return carry

    for g in range(2):
        lax.fori_loop(0, 16, functools.partial(read_labels, g=g), 0)

    total = (field[:96] + field[96:]) / (WEISSENBERG * DUMB)
    stress = [
        jnp.concatenate([total[16 * c : 16 * c + 8], total[16 * c + 8 : 16 * c + 16]], axis=1) for c in range(6)
    ]
    for k in range(3):
        sx[k] = stress[ALONG_X[k]]
        sy[k] = stress[ALONG_Y[k]]
        u, d = along_z(stress[ALONG_Z[k]])
        dv[ens, k] = 0.5 * (u - d)

    def stress_copy(slot):
        return pltpu.make_async_remote_copy(
            src_ref=sx if slot < 2 else sy, dst_ref=shx.at[slot] if slot < 2 else shy.at[slot - 2],
            send_sem=hs_sem.at[slot], recv_sem=hr_sem.at[slot],
            device_id=halo_targets[slot], device_id_type=MESH,
        )

    for slot in range(4):
        stress_copy(slot).start()

    noise_copy.wait()
    slot_lane = lax.broadcasted_iota(jnp.int32, (CAP, 128), 1).astype(F32)

    def arrive(j, carry, g):
        code_x, code_z = carry
        own = j == 0
        i = lax.rem(j + 15, 16)
        dx = jnp.where(own, 0, lax.rem(code_x, 4))
        dz = jnp.where(own, 0, lax.rem(code_z, 4))
        code_x = jnp.where(own, code_x, lax.div(code_x, 4))
        code_z = jnp.where(own, code_z, lax.div(code_z, 4))
        for r in range(2):
            pltpu.make_async_copy(recv.at[g, i, r], recv.at[g, i, r], rsem.at[g, i, r]).wait()
        for r in range(2):
            source = (lax.rem(my_x + 4 - dx, 4) * 2 + lax.rem(core + r, 2)) * 4 + lax.rem(cy + 4 - dz, 4)
            rows = pl.ds(pl.multiple_of(source * CAP, CAP), CAP)
            here = columns[g, i, r * 64 : r * 64 + CAP]
            live = slot_lane < here[:, 9:10]
            x = [jnp.where(live, recv[g, i, r, a], 0.0) for a in range(3)]
            inverse = 1.0 / (1.0 - (x[0] * x[0] + x[1] * x[1] + x[2] * x[2]) / EXTENSION)
            for a in range(3):
                stretch = sum(here[:, 3 * a + b : 3 * a + b + 1] * x[b] for b in range(3))
                stepped = (
                    x[a]
                    + TIME_STEP * (stretch - x[a] * inverse / (2.0 * WEISSENBERG))
                    + math.sqrt(TIME_STEP / WEISSENBERG) * noise[a, g, rows]
                )
                out_ref[a, g, rows] = jnp.where(live, stepped, 0.0)
        return code_x, code_z

    lax.fori_loop(0, 16, functools.partial(arrive, g=0), codes)

    for slot in range(4):
        stress_copy(slot).wait()
    for k in range(3):
        fx, fy = sx[k], sy[k]
        e, w, _, _ = stencil(fx, masked(shx[0, k], 0), masked(shx[1, k], 1), fx, fx)
        _, _, n, s = stencil(fy, fy, fy, masked(shy[0, k], 2), masked(shy[1, k], 3))
        dv[ens, k] = dv[ens, k] + 0.5 * (e - w) + 0.5 * (n - s)

    def dv_copy(k):
        return pltpu.make_async_remote_copy(
            src_ref=dv.at[ens], dst_ref=dv.at[ens], send_sem=ds_sem.at[k], recv_sem=dr_sem.at[k],
            device_id=(lax.rem(ens + k, n_ens), cx, cy), device_id_type=MESH,
        )

    def dv_arrival(k):
        source = lax.rem(ens + n_ens - k, n_ens)
        pltpu.make_async_copy(dv.at[source], dv.at[source], dr_sem.at[k]).wait()

    for k in range(1, n_ens):
        dv_copy(k).start()

    lax.fori_loop(0, 16, functools.partial(arrive, g=1), codes)

    for k in range(1, n_ens):
        dv_arrival(k)
    vout_ref[...] = base[...] + TIME_STEP * (dv[0] + dv[1] + dv[2] + dv[3])

    for k in range(1, n_ens):
        dv_copy(k).wait_send()

    def sent(i, carry):
        for g in range(2):
            for r in range(2):
                pltpu.make_async_copy(sendbuf.at[g, i, r], sendbuf.at[g, i, r], ssem.at[g, i, r]).wait()
                pltpu.make_async_copy(labsend.at[g, i, r], labsend.at[g, i, r], lssem.at[g, i, r]).wait()
        return carry

    lax.fori_loop(0, 15, sent, 0)
    for g in range(2):
        pltpu.make_async_copy(sendbuf.at[g, 15, 1], sendbuf.at[g, 15, 1], ssem.at[g, 15, 1]).wait()
        pltpu.make_async_copy(labsend.at[g, 15, 1], labsend.at[g, 15, 1], lssem.at[g, 15, 1]).wait()


def on_device(conformations, fill_counts, dest_slots, dest_cells, velocity, noise):
    _, groups, blocks, slots = conformations.shape
    vmem = pl.BlockSpec(memory_space=pltpu.VMEM)
    hbm = pl.BlockSpec(memory_space=pl.ANY)
    tile = velocity.shape
    arguments = (conformations, fill_counts, dest_slots, dest_cells, velocity, noise)
    dma = pltpu.SemaphoreType.DMA
    return pl.pallas_call(
        kernel,
        out_shape=(
            pltpu.VMEM(noise.shape, F32),
            pltpu.VMEM(velocity.shape, F32),
        ),
        in_specs=[hbm] * 6,
        out_specs=(vmem, vmem),
        scratch_shapes=[
            pltpu.VMEM(conformations.shape, F32),
            pltpu.VMEM(fill_counts.shape, jnp.int32),
            pltpu.VMEM(fill_counts.shape, jnp.int32),
            pltpu.VMEM(fill_counts.shape, jnp.int32),
            pltpu.VMEM(tile, F32),
            pltpu.VMEM(noise.shape, F32),
            pltpu.VMEM((groups, blocks, 3 * slots), BF16),
            pltpu.VMEM((groups, blocks, 3 * slots), BF16),
            pltpu.VMEM((groups, 16, 2, 3, CAP, slots), F32),
            pltpu.VMEM((groups, 16, 2, 3, CAP, slots), F32),
            pltpu.VMEM((groups, 16, blocks), BF16),
            pltpu.VMEM((groups, 16, 2, 4, 128), F32),
            pltpu.VMEM((groups, 16, 2, 4, 128), F32),
            pltpu.VMEM((groups, 16, 128, 16), F32),
            pltpu.VMEM((4,) + tile, F32),
            pltpu.VMEM((288, 128), BF16),
            pltpu.VMEM((16, 128), F32),
            pltpu.VMEM((128, 12 * 128), BF16),
            pltpu.VMEM((192, 128), F32),
            pltpu.VMEM(tile, F32),
            pltpu.VMEM(tile, F32),
            pltpu.VMEM((2,) + tile, F32),
            pltpu.VMEM((2,) + tile, F32),
            pltpu.VMEM((4,) + tile, F32),
            pltpu.VMEM(tile, F32),
            dma((2,)), dma((4,)), dma,
            dma((groups, 16, 2)), dma((groups, 16, 2)),
            dma((groups, 16, 2)), dma((groups, 16, 2)),
            dma((4,)), dma((4,)), dma((4,)), dma((4,)), dma((4,)), dma((4,)),
        ],
        compiler_params=pltpu.CompilerParams(
            collective_id=0, has_side_effects=True, vmem_limit_bytes=40 * 2**20
        ),
    )(*(pltpu.with_memory_space_constraint(x, pltpu.HBM) for x in arguments))


def solution(mesh):
    placed = (
        P(None, "ens", ("cx", "cy"), None),
        P("ens", ("cx", "cy")),
        P("ens", ("cx", "cy")),
        P("ens", ("cx", "cy")),
        P(None, "cx", "cy"),
        P(None, "ens", ("cx", "cy"), None),
    )
    return jax.shard_map(
        on_device,
        mesh=mesh,
        in_specs=placed,
        out_specs=(P(None, "ens", ("cx", "cy"), None), P(None, "cx", "cy")),
        check_vma=False,
    )
```

time: 89.4 us -> 81.6 us (0.913); the launches traced: 89.1 us -> 80.4 us
  local copies, waits for them, and re-layouts: 8.25 us -> 2.8 us
  Pallas kernels: 80.2 us -> 76.9 us
    unnamed x10 -> x2, local copies, waits for them, and re-layouts: 8.25 us -> 2.8 us
    pallas_call x1, Pallas kernels: 80.2 us -> 76.9 us  [on_device(): pl.pallas_call(kernel, out_shape=(pltpu.VMEM(noise.shape, F32), pltpu.VME...]
where the time goes in v2:
time: 81.6 us; the launch traced here: 80.4 us
  Pallas kernels  76.9 us (94%)
  local copies, waits for them, and re-layouts  2.8 us (3%)
    pallas_call x1, Pallas kernels, on_device(): pl.pallas_call(kernel, out_shape=(pltpu.VMEM(noise.shape, F32), pltpu.VME...  76.9 us
    unnamed x2, local copies, waits for them, and re-layouts  2.8 us

profile of v2, /device:TPU:1, one launch (start us, length us, event | category | flops | bytes accessed | tf_op | source)
XLA Modules:
  0.0 80.4 jit_solution(6474486138539665931)
XLA Ops:
  0.6 76.9 %shard_map.77 = (f32[3,2,1536,128]{3,2,1,0:T(8,128)S(1)}, f32[3,8,256]{2,1,0:T(8,128)S(1)}) custom-call(f32[3,2,1024,128]{3,2,1,0:T(8,128)} %conf_hbm.1, s32[2,1024]{1,0:T(2,128)} %fill_hbm.1, s32[2,1024]{1,0:T(2,128)} %dest_hbm.1, s32[2,1024]{1,0:T(2,128)} %cell_hbm.1, f32[3,8,256]{2,1,0:T(8,128)} %vel_hbm.1, f32[3,2,1536,128]{3,2,1,0:T(8,128)} %noise_hbm.1), custom_call_target="tpu_custom_call" | custom-call | tf_op jit(solution)/shard_map/pallas_call | solution.py:426
  77.6 2.2 %copy.10 = f32[3,2,1536,128]{3,2,1,0:T(8,128)} copy(f32[3,2,1536,128]{3,2,1,0:T(8,128)S(1)} %get-tuple-element.2) | data formatting | bytes 9437184
  79.8 0.6 copy.11

commit v3 on v2

--- a/solution.py
+++ b/solution.py
@@ -65,8 +65,8 @@
 def kernel(
     conf_hbm, fill_hbm, dest_hbm, cell_hbm, vel_hbm, noise_hbm,
     out_ref, vout_ref,
-    conf, fill_ref, dest_ref, cell_ref, vel_ref, noise, high, low, sendbuf, recv, labmat, labsend, labrecv, columns,
-    vhalo, table, rowbuf, prods, field, sx, sy, shx, shy, dv, base,
+    conf, fill_ref, dest_ref, cell_ref, vel_ref, noise, high, low, sendbuf, recv, labels, labsend, labrecv, columns,
+    vhalo, table, rowbuf, field, sx, sy, shx, shy, dv, base,
     conf_sem, in_sem, noise_sem, ssem, rsem, lssem, lrsem, vs_sem, vr_sem, hs_sem, hr_sem, ds_sem, dr_sem,
 ):
     ens = lax.axis_index("ens")
@@ -118,8 +118,6 @@
 
     blocks = conf.shape[2]
     row48 = lax.broadcasted_iota(jnp.int32, (CAP, blocks), 0)
-    row64 = lax.broadcasted_iota(jnp.int32, (64, blocks), 0)
-    row64 = jnp.where(row64 < CAP, row64, 2**20)
     lane128 = lax.broadcasted_iota(jnp.int32, (1, 128), 1)
 
     field[...] = jnp.zeros_like(field)
@@ -129,6 +127,16 @@
     for copy in small:
         copy.wait()
     pl.semaphore_wait(barrier, 31 + n_ens - 1)
+
+    def vel_copy(slot, target):
+        return pltpu.make_async_remote_copy(
+            src_ref=vel_ref, dst_ref=vhalo.at[slot], send_sem=vs_sem.at[slot], recv_sem=vr_sem.at[slot],
+            device_id=target, device_id_type=MESH,
+        )
+
+    halo_targets = (east_id, west_id, north_id, south_id)
+    for slot in range(4):
+        vel_copy(slot, halo_targets[slot]).start()
 
     def data_copy(g, i, r, h, target):
         rows = pl.ds(h * PART, PART)
@@ -193,83 +201,85 @@
         return carry
 
     codes = (jnp.int32(CODE_X), jnp.int32(CODE_Z))
-    later_codes = (jnp.int32(CODE_X // 4**8), jnp.int32(CODE_Z // 4**8))
-    lax.fori_loop(0, 2, functools.partial(pack_batch, g=0), codes)
-
-    def vel_copy(slot, target):
-        return pltpu.make_async_remote_copy(
-            src_ref=vel_ref, dst_ref=vhalo.at[slot], send_sem=vs_sem.at[slot], recv_sem=vr_sem.at[slot],
-            device_id=target, device_id_type=MESH,
-        )
-
-    halo_targets = (east_id, west_id, north_id, south_id)
-    for slot in range(4):
-        vel_copy(slot, halo_targets[slot]).start()
-
-    lab_row = lax.broadcasted_iota(jnp.int32, (16, 128), 0)
-    block_lane = lax.broadcasted_iota(jnp.int32, (128, 128), 1).astype(F32)
-    pick_row = lax.broadcasted_iota(jnp.int32, (16, 12 * 128), 0)
-    pick_pair = lax.div(lax.broadcasted_iota(jnp.int32, (16, 12 * 128), 1), 256)
-    pick = jnp.where((pick_row == pick_pair + 3) | (pick_row == pick_pair + 9), 1.0, 0.0).astype(BF16)
+
+    def send_blocks(g, first, last):
+        start = tuple(jnp.int32(code // 4 ** (4 * first)) for code in (CODE_X, CODE_Z))
+        lax.fori_loop(first, last, functools.partial(pack_batch, g=g), start)
+
+    send_blocks(0, 0, 1)
+
+    lab_row = lax.broadcasted_iota(jnp.int32, (8, 128), 0)
+    block_lane = lax.broadcasted_iota(jnp.int32, (128, 128), 1)
 
     def label_rows(k, carry, g):
         rows = pl.ds(pl.multiple_of(k * 128, 128), 128)
-        fill = fill_ref[g : g + 1, rows].astype(F32)
-        cell = cell_ref[g : g + 1, rows]
-        rowbuf[0:1] = fill
-        live = block_lane < rowbuf[...].T[:, 0:1]
+        fill = fill_ref[g : g + 1, rows]
+        cell = cell_ref[g : g + 1, rows].astype(F32)
+        live = block_lane < jnp.broadcast_to(fill, (8, 128)).T[:, 0:1]
+        fill = fill.astype(F32)
         x = [jnp.where(live, conf[a, g, rows], 0.0) for a in range(3)]
         inverse = 1.0 / (1.0 - (x[0] * x[0] + x[1] * x[1] + x[2] * x[2]) / EXTENSION)
         spring = [x[a] * inverse for a in range(3)]
+        sums = jnp.zeros((128, 128), F32)
         for c, (a, b) in enumerate(PAIRS):
-            first, second = halves_of(x[a] * spring[b])
-            prods[:, c * 256 : c * 256 + 128] = first
-            prods[:, c * 256 + 128 : c * 256 + 256] = second
-        sums = lax.dot_general(pick, prods[...], NT, preferred_element_type=F32)
-        first = sums.astype(BF16).astype(F32)
-        cell_hi = lax.div(cell, 128).astype(F32)
-        cell_lo = lax.rem(cell, 128).astype(F32)
-        rest = jnp.where(lab_row < 9, first, jnp.where(lab_row < 15, sums - first, 0.0))
-        labmat[g, :, rows] = jnp.where(
-            lab_row == 0, fill, jnp.where(lab_row == 1, cell_hi, jnp.where(lab_row == 2, cell_lo, rest))
-        ).astype(BF16)
+            sums = jnp.where(block_lane == c + 2, jnp.sum(x[a] * spring[b], axis=1, keepdims=True), sums)
+        sums = sums.T[:8]
+        labels[g, :, rows] = jnp.where(lab_row == 0, fill, jnp.where(lab_row == 1, cell, sums))
         return carry
 
     conf_copy(1).wait()
     for g in range(2):
         lax.fori_loop(0, blocks // 128, functools.partial(label_rows, g=g), 0)
 
-    def label_batch(q, carry, g):
-        targets, carry = batch_targets(carry)
-        onehot = one_hot(dest_ref[g : g + 1, :], targets, row64)
-        told = lax.dot_general(labmat[g], onehot, NT, preferred_element_type=F32)
-        top = jnp.concatenate([told[0:1], told[1:2] * 128.0 + told[2:3], told[3:5] + told[9:11]], axis=0)
-        bottom = told[5:9] + told[11:15]
-        for m in range(4):
-            upper, lower = top[:, m * 128 : (m + 1) * 128], bottom[:, m * 128 : (m + 1) * 128]
-            labsend[g, 4 * q + m, 0] = jnp.where(lane128 < 64, upper, pltpu.roll(lower, 64, 1))
-            labsend[g, 4 * q + m, 1] = jnp.where(lane128 < 64, pltpu.roll(upper, 64, 1), lower)
-        for n in range(6):
-            label_copy(g, 4 * q + n // 2, n % 2, targets[n]).start()
-
-        @pl.when(q < 3)
-        def _():
-            for n in range(6, 8):
-                label_copy(g, 4 * q + n // 2, n % 2, targets[n]).start()
-
-        @pl.when(q == 3)
-        def _():
-            label_copy(g, 15, 1, targets[7]).start()
-            pltpu.make_async_copy(labsend.at[g, 15, 0], labrecv.at[g, 15, 0], lrsem.at[g, 15, 0]).start()
-
-        return carry
+    row8 = lax.broadcasted_iota(jnp.int32, (8, blocks), 0)
+    row128 = lax.broadcasted_iota(jnp.int32, (128, blocks), 0)
+
+    def send_labels(g):
+        dest = dest_ref[g : g + 1, :]
+        owner = ((dest.astype(F32) + 0.5) * (1.0 / CAP)).astype(jnp.int32)
+        slot = dest - owner * CAP
+        values = labels[g]
+        first = values.astype(BF16).astype(F32)
+        terms = (first, values - first)
+        told = jnp.zeros((128, 128), F32)
+        chips = []
+        for p in range(16):
+            (_, x0, z0), (_, x1, _) = chip(p // 4, p % 4, 0), chip(p // 4, p % 4, 1)
+            chips.append(owner == jnp.where(row8 < 4, x0 * 4 + z0, x1 * 4 + z0))
+        for half in range(2):
+            where_to = jnp.where(row128 - 64 * half == slot, 1.0, 0.0).astype(BF16)
+            for term in terms:
+                four = term[4 * half : 4 * half + 4]
+                four = jnp.concatenate([four, four], axis=0)
+                spread = jnp.concatenate(
+                    [
+                        jnp.concatenate(
+                            [jnp.where(chips[p], four, 0.0), jnp.where(chips[p + 1], four, 0.0)], axis=0
+                        ).astype(BF16)
+                        for p in range(0, 16, 2)
+                    ],
+                    axis=0,
+                )
+                told = told + lax.dot_general(spread, where_to, NT, preferred_element_type=F32)
+        for p in range(16):
+            for r in range(2):
+                labsend[g, p, r] = told[8 * p + 4 * r : 8 * p + 4 * r + 4]
+        label_copy(g, 0, 1, chip(0, 0, 1)).start()
+        pltpu.make_async_copy(labsend.at[g, 0, 0], labrecv.at[g, 0, 0], lrsem.at[g, 0, 0]).start()
+
+        def start(p, carry):
+            for r in range(2):
+                label_copy(g, p, r, chip(lax.div(p, 4), lax.rem(p, 4), r)).start()
+            return carry
+
+        lax.fori_loop(1, 16, start, 0)
 
     for g in range(2):
-        lax.fori_loop(0, 4, functools.partial(label_batch, g=g), codes)
-
-    lax.fori_loop(2, 4, functools.partial(pack_batch, g=0), later_codes)
+        send_labels(g)
+
+    send_blocks(0, 1, 4)
     split(1)
-    lax.fori_loop(0, 4, functools.partial(pack_batch, g=1), codes)
+    send_blocks(1, 0, 1)
 
     for slot in range(4):
         vel_copy(slot, halo_targets[slot]).wait()
@@ -292,34 +302,44 @@
     square = lax.broadcasted_iota(jnp.int32, (128, 128), 0)
     row_hi = lax.broadcasted_iota(jnp.int32, (16, 128), 0)
 
-    def read_labels(i, carry, g):
-        for r in range(2):
-            pltpu.make_async_copy(labrecv.at[g, i, r], labrecv.at[g, i, r], lrsem.at[g, i, r]).wait()
-        lab0, lab1 = labrecv[g, i, 0], labrecv[g, i, 1]
-        upper = jnp.where(lane128 < 64, lab0, pltpu.roll(lab1, 64, 1))
-        lower = jnp.where(lane128 < 64, pltpu.roll(lab0, 64, 1), lab1)
-        cells = upper[1:2].astype(jnp.int32)
-        cell_lo = lax.rem(cells, 128)
-        cell_hi = lax.div(cells, 128)
-        cell_hi = lax.rem(cell_hi, 2) * 8 + lax.div(cell_hi, 2)
-        at_lo = jnp.where(square == cell_lo, 1.0, 0.0).astype(BF16)
-        at_hi = jnp.where(row_hi == cell_hi, 1.0, 0.0)
-        looked = jnp.dot(table[...], at_lo, preferred_element_type=F32)
-        looked = looked[:144] + looked[144:]
-        for c in range(9):
-            rowbuf[c : c + 1] = jnp.sum(looked[16 * c : 16 * c + 16] * at_hi, axis=0, keepdims=True)
-        rowbuf[9:10] = upper[0:1]
-        columns[g, i] = rowbuf[...].T
-        sums = [upper[2:3], upper[3:4]] + [lower[c : c + 1] for c in range(4)]
-        spread = jnp.concatenate([sums[c] * at_hi for c in range(6)], axis=0)
+    def read_labels(q, carry, g):
+        uppers, sums, lows, highs = [], [], [], []
+        for m in range(4):
+            for r in range(2):
+                landed = labrecv.at[g, 4 * q + m, r]
+                pltpu.make_async_copy(landed, landed, lrsem.at[g, 4 * q + m, r]).wait()
+            lab0, lab1 = labrecv[g, 4 * q + m, 0], labrecv[g, 4 * q + m, 1]
+            upper = jnp.where(lane128 < 64, lab0, pltpu.roll(lab1, 64, 1))
+            lower = jnp.where(lane128 < 64, pltpu.roll(lab0, 64, 1), lab1)
+            cells = upper[1:2].astype(jnp.int32)
+            cell_hi = lax.div(cells, 128)
+            cell_hi = lax.rem(cell_hi, 2) * 8 + lax.div(cell_hi, 2)
+            uppers.append(upper)
+            sums.append([upper[2:3], upper[3:4]] + [lower[c : c + 1] for c in range(4)])
+            lows.append(jnp.where(square == lax.rem(cells, 128), 1.0, 0.0).astype(BF16))
+            highs.append(jnp.where(row_hi == cell_hi, 1.0, 0.0))
+        at_lo = jnp.concatenate(lows, axis=1)
+        spread = jnp.concatenate(
+            [jnp.concatenate([sums[m][c] * highs[m] for c in range(6)], axis=0) for m in range(4)], axis=1
+        )
         first, second = halves_of(spread)
         field[...] += lax.dot_general(
             jnp.concatenate([first, second], axis=0), at_lo, NT, preferred_element_type=F32
         )
+        looked = jnp.dot(table[...], at_lo, preferred_element_type=F32)
+        looked = looked[:144] + looked[144:]
+        for m in range(4):
+            for c in range(9):
+                rowbuf[m, c : c + 1] = jnp.sum(
+                    looked[16 * c : 16 * c + 16, 128 * m : 128 * m + 128] * highs[m], axis=0, keepdims=True
+                )
+            rowbuf[m, 9:10] = uppers[m][0:1]
+        for m in range(4):
+            columns[g, 4 * q + m] = rowbuf[m].T
         return carry
 
     for g in range(2):
-        lax.fori_loop(0, 16, functools.partial(read_labels, g=g), 0)
+        lax.fori_loop(0, 4, functools.partial(read_labels, g=g), 0)
 
     total = (field[:96] + field[96:]) / (WEISSENBERG * DUMB)
     stress = [
@@ -341,6 +361,29 @@
     for slot in range(4):
         stress_copy(slot).start()
 
+    for slot in range(4):
+        stress_copy(slot).wait()
+    for k in range(3):
+        fx, fy = sx[k], sy[k]
+        e, w, _, _ = stencil(fx, masked(shx[0, k], 0), masked(shx[1, k], 1), fx, fx)
+        _, _, n, s = stencil(fy, fy, fy, masked(shy[0, k], 2), masked(shy[1, k], 3))
+        dv[ens, k] = dv[ens, k] + 0.5 * (e - w) + 0.5 * (n - s)
+
+    def dv_copy(k):
+        return pltpu.make_async_remote_copy(
+            src_ref=dv.at[ens], dst_ref=dv.at[ens], send_sem=ds_sem.at[k], recv_sem=dr_sem.at[k],
+            device_id=(lax.rem(ens + k, n_ens), cx, cy), device_id_type=MESH,
+        )
+
+    def dv_arrival(k):
+        source = lax.rem(ens + n_ens - k, n_ens)
+        pltpu.make_async_copy(dv.at[source], dv.at[source], dr_sem.at[k]).wait()
+
+    for k in range(1, n_ens):
+        dv_copy(k).start()
+
+
+    send_blocks(1, 1, 4)
     noise_copy.wait()
     slot_lane = lax.broadcasted_iota(jnp.int32, (CAP, 128), 1).astype(F32)
 
@@ -357,7 +400,7 @@
         for r in range(2):
             source = (lax.rem(my_x + 4 - dx, 4) * 2 + lax.rem(core + r, 2)) * 4 + lax.rem(cy + 4 - dz, 4)
             rows = pl.ds(pl.multiple_of(source * CAP, CAP), CAP)
-            here = columns[g, i, r * 64 : r * 64 + CAP]
+            here = columns[g, dx * 4 + dz, r * 64 : r * 64 + CAP]
             live = slot_lane < here[:, 9:10]
             x = [jnp.where(live, recv[g, i, r, a], 0.0) for a in range(3)]
             inverse = 1.0 / (1.0 - (x[0] * x[0] + x[1] * x[1] + x[2] * x[2]) / EXTENSION)
@@ -373,27 +416,6 @@
 
     lax.fori_loop(0, 16, functools.partial(arrive, g=0), codes)
 
-    for slot in range(4):
-        stress_copy(slot).wait()
-    for k in range(3):
-        fx, fy = sx[k], sy[k]
-        e, w, _, _ = stencil(fx, masked(shx[0, k], 0), masked(shx[1, k], 1), fx, fx)
-        _, _, n, s = stencil(fy, fy, fy, masked(shy[0, k], 2), masked(shy[1, k], 3))
-        dv[ens, k] = dv[ens, k] + 0.5 * (e - w) + 0.5 * (n - s)
-
-    def dv_copy(k):
-        return pltpu.make_async_remote_copy(
-            src_ref=dv.at[ens], dst_ref=dv.at[ens], send_sem=ds_sem.at[k], recv_sem=dr_sem.at[k],
-            device_id=(lax.rem(ens + k, n_ens), cx, cy), device_id_type=MESH,
-        )
-
-    def dv_arrival(k):
-        source = lax.rem(ens + n_ens - k, n_ens)
-        pltpu.make_async_copy(dv.at[source], dv.at[source], dr_sem.at[k]).wait()
-
-    for k in range(1, n_ens):
-        dv_copy(k).start()
-
     lax.fori_loop(0, 16, functools.partial(arrive, g=1), codes)
 
     for k in range(1, n_ens):
@@ -407,13 +429,14 @@
         for g in range(2):
             for r in range(2):
                 pltpu.make_async_copy(sendbuf.at[g, i, r], sendbuf.at[g, i, r], ssem.at[g, i, r]).wait()
-                pltpu.make_async_copy(labsend.at[g, i, r], labsend.at[g, i, r], lssem.at[g, i, r]).wait()
+                told = labsend.at[g, i + 1, r]
+                pltpu.make_async_copy(told, told, lssem.at[g, i + 1, r]).wait()
         return carry
 
     lax.fori_loop(0, 15, sent, 0)
     for g in range(2):
         pltpu.make_async_copy(sendbuf.at[g, 15, 1], sendbuf.at[g, 15, 1], ssem.at[g, 15, 1]).wait()
-        pltpu.make_async_copy(labsend.at[g, 15, 1], labsend.at[g, 15, 1], lssem.at[g, 15, 1]).wait()
+        pltpu.make_async_copy(labsend.at[g, 0, 1], labsend.at[g, 0, 1], lssem.at[g, 0, 1]).wait()
 
 
 def on_device(conformations, fill_counts, dest_slots, dest_cells, velocity, noise):
@@ -442,14 +465,13 @@
             pltpu.VMEM((groups, blocks, 3 * slots), BF16),
             pltpu.VMEM((groups, 16, 2, 3, CAP, slots), F32),
             pltpu.VMEM((groups, 16, 2, 3, CAP, slots), F32),
-            pltpu.VMEM((groups, 16, blocks), BF16),
+            pltpu.VMEM((groups, 8, blocks), F32),
             pltpu.VMEM((groups, 16, 2, 4, 128), F32),
             pltpu.VMEM((groups, 16, 2, 4, 128), F32),
             pltpu.VMEM((groups, 16, 128, 16), F32),
             pltpu.VMEM((4,) + tile, F32),
             pltpu.VMEM((288, 128), BF16),
-            pltpu.VMEM((16, 128), F32),
-            pltpu.VMEM((128, 12 * 128), BF16),
+            pltpu.VMEM((4, 16, 128), F32),
             pltpu.VMEM((192, 128), F32),
             pltpu.VMEM(tile, F32),
             pltpu.VMEM(tile, F32),

time: 81.6 us -> 75.2 us (0.922); the launches traced: 80.4 us -> 75.1 us
  Pallas kernels: 76.9 us -> 71.7 us
    pallas_call x1, Pallas kernels: 76.9 us -> 71.7 us  [on_device(): pl.pallas_call(kernel, out_shape=(pltpu.VMEM(noise.shape, F32), pltpu.VME...]
where the time goes in v3:
time: 75.2 us; the launch traced here: 75.1 us
  Pallas kernels  71.7 us (95%)
  local copies, waits for them, and re-layouts  2.8 us (4%)
    pallas_call x1, Pallas kernels, on_device(): pl.pallas_call(kernel, out_shape=(pltpu.VMEM(noise.shape, F32), pltpu.VME...  71.7 us
    unnamed x2, local copies, waits for them, and re-layouts  2.8 us

profile of v3, /device:TPU:1, one launch (start us, length us, event | category | flops | bytes accessed | tf_op | source)
XLA Modules:
  0.0 75.1 jit_solution(8329474758970363985)
XLA Ops:
  0.6 71.7 %shard_map.77 = (f32[3,2,1536,128]{3,2,1,0:T(8,128)S(1)}, f32[3,8,256]{2,1,0:T(8,128)S(1)}) custom-call(f32[3,2,1024,128]{3,2,1,0:T(8,128)} %conf_hbm.1, s32[2,1024]{1,0:T(2,128)} %fill_hbm.1, s32[2,1024]{1,0:T(2,128)} %dest_hbm.1, s32[2,1024]{1,0:T(2,128)} %cell_hbm.1, f32[3,8,256]{2,1,0:T(8,128)} %vel_hbm.1, f32[3,2,1536,128]{3,2,1,0:T(8,128)} %noise_hbm.1), custom_call_target="tpu_custom_call" | custom-call | tf_op jit(solution)/shard_map/pallas_call | solution.py:449
  72.3 2.2 %copy.10 = f32[3,2,1536,128]{3,2,1,0:T(8,128)} copy(f32[3,2,1536,128]{3,2,1,0:T(8,128)S(1)} %get-tuple-element.2) | data formatting | bytes 9437184
  74.5 0.6 copy.11

commit v4 on v3

--- a/solution.py
+++ b/solution.py
@@ -88,9 +88,7 @@
     conf_copy(0).start()
     for copy in small:
         copy.start()
-    conf_copy(1).start()
     noise_copy = pltpu.make_async_copy(noise_hbm, noise, noise_sem)
-    noise_copy.start()
 
     east_id = (ens, lax.rem(cx + 1, 8), cy)
     west_id = (ens, lax.rem(cx + 7, 8), cy)
@@ -123,6 +121,7 @@
     field[...] = jnp.zeros_like(field)
     rowbuf[...] = jnp.zeros_like(rowbuf)
     conf_copy(0).wait()
+    conf_copy(1).start()
     split(0)
     for copy in small:
         copy.wait()
@@ -138,75 +137,74 @@
     for slot in range(4):
         vel_copy(slot, halo_targets[slot]).start()
 
-    def data_copy(g, i, r, h, target):
+    def data_copy(g, i, p, r, h, target):
         rows = pl.ds(h * PART, PART)
         return pltpu.make_async_remote_copy(
-            src_ref=sendbuf.at[g, i, r, :, rows], dst_ref=recv.at[g, i, r, :, rows],
-            send_sem=ssem.at[g, i, r], recv_sem=rsem.at[g, i, r],
+            src_ref=sendbuf.at[g, i, r, :, rows], dst_ref=recv.at[g, p, r, :, rows],
+            send_sem=ssem.at[g, i, r], recv_sem=rsem.at[g, p, r],
             device_id=target, device_id_type=MESH,
         )
 
-    def label_copy(g, i, r, target):
+    def label_copy(p, r, target):
         return pltpu.make_async_remote_copy(
-            src_ref=labsend.at[g, i, r], dst_ref=labrecv.at[g, i, r],
-            send_sem=lssem.at[g, i, r], recv_sem=lrsem.at[g, i, r],
+            src_ref=labsend.at[p, r], dst_ref=labrecv.at[p, r],
+            send_sem=lssem.at[p, r], recv_sem=lrsem.at[p, r],
             device_id=target, device_id_type=MESH,
         )
 
-    def batch_targets(carry):
+    def pack_batch(q, carry, g, width):
         code_x, code_z = carry
-        targets = []
-        for _ in range(4):
+        targets, landing = [], []
+        for _ in range(width):
             dx, dz = lax.rem(code_x, 4), lax.rem(code_z, 4)
             code_x, code_z = lax.div(code_x, 4), lax.div(code_z, 4)
+            dx = jnp.where(core == 0, dx, lax.rem(4 - dx, 4))
+            dz = jnp.where(core == 0, dz, lax.rem(4 - dz, 4))
+            landing.append(dx * 4 + dz)
             targets += [chip(dx, dz, 0), chip(dx, dz, 1)]
-        return targets, (code_x, code_z)
-
-    def one_hot(dest, targets, rows):
-        return jnp.concatenate(
+        dest = dest_ref[g : g + 1, :]
+        onehot = jnp.concatenate(
             [
-                jnp.where(dest - (target[1] * 4 + target[2]) * CAP == rows, 1.0, 0.0).astype(BF16)
+                jnp.where(dest - (target[1] * 4 + target[2]) * CAP == row48, 1.0, 0.0).astype(BF16)
                 for target in targets
             ],
             axis=0,
         )
-
-    def pack_batch(q, carry, g):
-        targets, carry = batch_targets(carry)
-        onehot = one_hot(dest_ref[g : g + 1, :], targets, row48)
         packed = jnp.dot(onehot, high[g], preferred_element_type=F32) + jnp.dot(
             onehot, low[g], preferred_element_type=F32
         )
-        for n in range(8):
+        for n in range(2 * width):
             for a in range(3):
-                sendbuf[g, 4 * q + n // 2, n % 2, a] = packed[
+                sendbuf[g, width * q + n // 2, n % 2, a] = packed[
                     n * CAP : (n + 1) * CAP, a * 128 : (a + 1) * 128
                 ]
-        for h in range(HALVES):
-            for n in range(6):
-                data_copy(g, 4 * q + n // 2, n % 2, h, targets[n]).start()
-
-        @pl.when(q < 3)
+
+        def start(first, last):
+            for h in range(HALVES):
+                for n in range(first, last):
+                    data_copy(g, width * q + n // 2, landing[n // 2], n % 2, h, targets[n]).start()
+
+        start(0, 2 * width - 2)
+
+        @pl.when(q < 16 // width - 1)
         def _():
-            for h in range(HALVES):
-                for n in range(6, 8):
-                    data_copy(g, 4 * q + n // 2, n % 2, h, targets[n]).start()
-
-        @pl.when(q == 3)
+            start(2 * width - 2, 2 * width)
+
+        @pl.when(q == 16 // width - 1)
         def _():
-            for h in range(HALVES):
-                data_copy(g, 15, 1, h, targets[7]).start()
-            pltpu.make_async_copy(sendbuf.at[g, 15, 0], recv.at[g, 15, 0], rsem.at[g, 15, 0]).start()
-
-        return carry
+            start(2 * width - 1, 2 * width)
+            pltpu.make_async_copy(sendbuf.at[g, 15, 0], recv.at[g, 0, 0], rsem.at[g, 0, 0]).start()
+
+        return code_x, code_z
 
     codes = (jnp.int32(CODE_X), jnp.int32(CODE_Z))
 
-    def send_blocks(g, first, last):
-        start = tuple(jnp.int32(code // 4 ** (4 * first)) for code in (CODE_X, CODE_Z))
-        lax.fori_loop(first, last, functools.partial(pack_batch, g=g), start)
-
-    send_blocks(0, 0, 1)
+    def send_blocks(g, first, last, width=4):
+        start = tuple(jnp.int32(code // 4 ** (width * first)) for code in (CODE_X, CODE_Z))
+        lax.fori_loop(first, last, functools.partial(pack_batch, g=g, width=width), start)
+
+    send_blocks(0, 0, 2, width=2)
+    send_blocks(0, 1, 2)
 
     lab_row = lax.broadcasted_iota(jnp.int32, (8, 128), 0)
     block_lane = lax.broadcasted_iota(jnp.int32, (128, 128), 1)
@@ -228,58 +226,55 @@
         return carry
 
     conf_copy(1).wait()
+    noise_copy.start()
     for g in range(2):
         lax.fori_loop(0, blocks // 128, functools.partial(label_rows, g=g), 0)
 
-    row8 = lax.broadcasted_iota(jnp.int32, (8, blocks), 0)
     row128 = lax.broadcasted_iota(jnp.int32, (128, blocks), 0)
 
-    def send_labels(g):
-        dest = dest_ref[g : g + 1, :]
-        owner = ((dest.astype(F32) + 0.5) * (1.0 / CAP)).astype(jnp.int32)
-        slot = dest - owner * CAP
-        values = labels[g]
-        first = values.astype(BF16).astype(F32)
-        terms = (first, values - first)
-        told = jnp.zeros((128, 128), F32)
-        chips = []
-        for p in range(16):
-            (_, x0, z0), (_, x1, _) = chip(p // 4, p % 4, 0), chip(p // 4, p % 4, 1)
-            chips.append(owner == jnp.where(row8 < 4, x0 * 4 + z0, x1 * 4 + z0))
-        for half in range(2):
-            where_to = jnp.where(row128 - 64 * half == slot, 1.0, 0.0).astype(BF16)
-            for term in terms:
-                four = term[4 * half : 4 * half + 4]
-                four = jnp.concatenate([four, four], axis=0)
+    def send_labels():
+        told = jnp.zeros((256, 128), F32)
+        for g in range(2):
+            dest = dest_ref[g : g + 1, :]
+            owner = ((dest.astype(F32) + 0.5) * (1.0 / CAP)).astype(jnp.int32)
+            slot = dest - owner * CAP
+            where_to = jnp.where(row128 - 64 * g == slot, 1.0, 0.0).astype(BF16)
+            values = labels[g]
+            first = values.astype(BF16).astype(F32)
+            masks = []
+            for p in range(16):
+                for r in range(2):
+                    _, x, z = chip(p // 4, p % 4, r)
+                    masks.append(jnp.broadcast_to(owner == x * 4 + z, values.shape))
+            for term in (first, values - first):
                 spread = jnp.concatenate(
                     [
                         jnp.concatenate(
-                            [jnp.where(chips[p], four, 0.0), jnp.where(chips[p + 1], four, 0.0)], axis=0
+                            [jnp.where(masks[n], term, 0.0), jnp.where(masks[n + 1], term, 0.0)], axis=0
                         ).astype(BF16)
-                        for p in range(0, 16, 2)
+                        for n in range(0, 32, 2)
                     ],
                     axis=0,
                 )
                 told = told + lax.dot_general(spread, where_to, NT, preferred_element_type=F32)
         for p in range(16):
             for r in range(2):
-                labsend[g, p, r] = told[8 * p + 4 * r : 8 * p + 4 * r + 4]
-        label_copy(g, 0, 1, chip(0, 0, 1)).start()
-        pltpu.make_async_copy(labsend.at[g, 0, 0], labrecv.at[g, 0, 0], lrsem.at[g, 0, 0]).start()
+                labsend[p, r] = told[16 * p + 8 * r : 16 * p + 8 * r + 8]
+        label_copy(0, 1, chip(0, 0, 1)).start()
+        pltpu.make_async_copy(labsend.at[0, 0], labrecv.at[0, 0], lrsem.at[0, 0]).start()
 
         def start(p, carry):
             for r in range(2):
-                label_copy(g, p, r, chip(lax.div(p, 4), lax.rem(p, 4), r)).start()
+                label_copy(p, r, chip(lax.div(p, 4), lax.rem(p, 4), r)).start()
             return carry
 
         lax.fori_loop(1, 16, start, 0)
 
-    for g in range(2):
-        send_labels(g)
-
-    send_blocks(0, 1, 4)
+    send_labels()
+
+    send_blocks(0, 2, 4)
     split(1)
-    send_blocks(1, 0, 1)
+    send_blocks(1, 0, 2)
 
     for slot in range(4):
         vel_copy(slot, halo_targets[slot]).wait()
@@ -303,24 +298,26 @@
     row_hi = lax.broadcasted_iota(jnp.int32, (16, 128), 0)
 
     def read_labels(q, carry, g):
-        uppers, sums, lows, highs = [], [], [], []
+        told, lows, highs = [], [], []
         for m in range(4):
-            for r in range(2):
-                landed = labrecv.at[g, 4 * q + m, r]
-                pltpu.make_async_copy(landed, landed, lrsem.at[g, 4 * q + m, r]).wait()
-            lab0, lab1 = labrecv[g, 4 * q + m, 0], labrecv[g, 4 * q + m, 1]
-            upper = jnp.where(lane128 < 64, lab0, pltpu.roll(lab1, 64, 1))
-            lower = jnp.where(lane128 < 64, pltpu.roll(lab0, 64, 1), lab1)
-            cells = upper[1:2].astype(jnp.int32)
+            p = 4 * q + m
+            if g == 0:
+                for r in range(2):
+                    pltpu.make_async_copy(labrecv.at[p, r], labrecv.at[p, r], lrsem.at[p, r]).wait()
+            lab0, lab1 = labrecv[p, 0], labrecv[p, 1]
+            if g == 0:
+                here = jnp.where(lane128 < 64, lab0, pltpu.roll(lab1, 64, 1))
+            else:
+                here = jnp.where(lane128 < 64, pltpu.roll(lab0, 64, 1), lab1)
+            cells = here[1:2].astype(jnp.int32)
             cell_hi = lax.div(cells, 128)
             cell_hi = lax.rem(cell_hi, 2) * 8 + lax.div(cell_hi, 2)
-            uppers.append(upper)
-            sums.append([upper[2:3], upper[3:4]] + [lower[c : c + 1] for c in range(4)])
+            told.append(here)
             lows.append(jnp.where(square == lax.rem(cells, 128), 1.0, 0.0).astype(BF16))
             highs.append(jnp.where(row_hi == cell_hi, 1.0, 0.0))
         at_lo = jnp.concatenate(lows, axis=1)
         spread = jnp.concatenate(
-            [jnp.concatenate([sums[m][c] * highs[m] for c in range(6)], axis=0) for m in range(4)], axis=1
+            [jnp.concatenate([told[m][c + 2 : c + 3] * highs[m] for c in range(6)], axis=0) for m in range(4)], axis=1
         )
         first, second = halves_of(spread)
         field[...] += lax.dot_general(
@@ -333,7 +330,7 @@
                 rowbuf[m, c : c + 1] = jnp.sum(
                     looked[16 * c : 16 * c + 16, 128 * m : 128 * m + 128] * highs[m], axis=0, keepdims=True
                 )
-            rowbuf[m, 9:10] = uppers[m][0:1]
+            rowbuf[m, 9:10] = told[m][0:1]
         for m in range(4):
             columns[g, 4 * q + m] = rowbuf[m].T
         return carry
@@ -361,29 +358,7 @@
     for slot in range(4):
         stress_copy(slot).start()
 
-    for slot in range(4):
-        stress_copy(slot).wait()
-    for k in range(3):
-        fx, fy = sx[k], sy[k]
-        e, w, _, _ = stencil(fx, masked(shx[0, k], 0), masked(shx[1, k], 1), fx, fx)
-        _, _, n, s = stencil(fy, fy, fy, masked(shy[0, k], 2), masked(shy[1, k], 3))
-        dv[ens, k] = dv[ens, k] + 0.5 * (e - w) + 0.5 * (n - s)
-
-    def dv_copy(k):
-        return pltpu.make_async_remote_copy(
-            src_ref=dv.at[ens], dst_ref=dv.at[ens], send_sem=ds_sem.at[k], recv_sem=dr_sem.at[k],
-            device_id=(lax.rem(ens + k, n_ens), cx, cy), device_id_type=MESH,
-        )
-
-    def dv_arrival(k):
-        source = lax.rem(ens + n_ens - k, n_ens)
-        pltpu.make_async_copy(dv.at[source], dv.at[source], dr_sem.at[k]).wait()
-
-    for k in range(1, n_ens):
-        dv_copy(k).start()
-
-
-    send_blocks(1, 1, 4)
+    send_blocks(1, 2, 4)
     noise_copy.wait()
     slot_lane = lax.broadcasted_iota(jnp.int32, (CAP, 128), 1).astype(F32)
 
@@ -395,14 +370,22 @@
         dz = jnp.where(own, 0, lax.rem(code_z, 4))
         code_x = jnp.where(own, code_x, lax.div(code_x, 4))
         code_z = jnp.where(own, code_z, lax.div(code_z, 4))
+        def sent(r):
+            pltpu.make_async_copy(sendbuf.at[g, i, r], sendbuf.at[g, i, r], ssem.at[g, i, r]).wait()
+            if g == 0:
+                pltpu.make_async_copy(labsend.at[j, r], labsend.at[j, r], lssem.at[j, r]).wait()
+
+        pl.when(j > 0)(lambda: sent(0))
+        sent(1)
         for r in range(2):
-            pltpu.make_async_copy(recv.at[g, i, r], recv.at[g, i, r], rsem.at[g, i, r]).wait()
+            landed = recv.at[g, dx * 4 + dz, r]
+            pltpu.make_async_copy(landed, landed, rsem.at[g, dx * 4 + dz, r]).wait()
         for r in range(2):
             source = (lax.rem(my_x + 4 - dx, 4) * 2 + lax.rem(core + r, 2)) * 4 + lax.rem(cy + 4 - dz, 4)
             rows = pl.ds(pl.multiple_of(source * CAP, CAP), CAP)
             here = columns[g, dx * 4 + dz, r * 64 : r * 64 + CAP]
             live = slot_lane < here[:, 9:10]
-            x = [jnp.where(live, recv[g, i, r, a], 0.0) for a in range(3)]
+            x = [jnp.where(live, recv[g, dx * 4 + dz, r, a], 0.0) for a in range(3)]
             inverse = 1.0 / (1.0 - (x[0] * x[0] + x[1] * x[1] + x[2] * x[2]) / EXTENSION)
             for a in range(3):
                 stretch = sum(here[:, 3 * a + b : 3 * a + b + 1] * x[b] for b in range(3))
@@ -415,6 +398,27 @@
         return code_x, code_z
 
     lax.fori_loop(0, 16, functools.partial(arrive, g=0), codes)
+    for slot in range(4):
+        stress_copy(slot).wait()
+    for k in range(3):
+        fx, fy = sx[k], sy[k]
+        e, w, _, _ = stencil(fx, masked(shx[0, k], 0), masked(shx[1, k], 1), fx, fx)
+        _, _, n, s = stencil(fy, fy, fy, masked(shy[0, k], 2), masked(shy[1, k], 3))
+        dv[ens, k] = dv[ens, k] + 0.5 * (e - w) + 0.5 * (n - s)
+
+    def dv_copy(k):
+        return pltpu.make_async_remote_copy(
+            src_ref=dv.at[ens], dst_ref=dv.at[ens], send_sem=ds_sem.at[k], recv_sem=dr_sem.at[k],
+            device_id=(lax.rem(ens + k, n_ens), cx, cy), device_id_type=MESH,
+        )
+
+    def dv_arrival(k):
+        source = lax.rem(ens + n_ens - k, n_ens)
+        pltpu.make_async_copy(dv.at[source], dv.at[source], dr_sem.at[k]).wait()
+
+    for k in range(1, n_ens):
+        dv_copy(k).start()
+
 
     lax.fori_loop(0, 16, functools.partial(arrive, g=1), codes)
 
@@ -425,18 +429,16 @@
     for k in range(1, n_ens):
         dv_copy(k).wait_send()
 
-    def sent(i, carry):
+
+def finish(conf_vmem, velocity_vmem, conf_hbm, velocity_hbm, sems):
+    copies = [pltpu.make_async_copy(velocity_vmem, velocity_hbm, sems.at[6])]
+    for a in range(3):
         for g in range(2):
-            for r in range(2):
-                pltpu.make_async_copy(sendbuf.at[g, i, r], sendbuf.at[g, i, r], ssem.at[g, i, r]).wait()
-                told = labsend.at[g, i + 1, r]
-                pltpu.make_async_copy(told, told, lssem.at[g, i + 1, r]).wait()
-        return carry
-
-    lax.fori_loop(0, 15, sent, 0)
-    for g in range(2):
-        pltpu.make_async_copy(sendbuf.at[g, 15, 1], sendbuf.at[g, 15, 1], ssem.at[g, 15, 1]).wait()
-        pltpu.make_async_copy(labsend.at[g, 0, 1], labsend.at[g, 0, 1], lssem.at[g, 0, 1]).wait()
+            copies.append(pltpu.make_async_copy(conf_vmem.at[a, g], conf_hbm.at[a, g], sems.at[2 * a + g]))
+    for copy in copies:
+        copy.start()
+    for copy in copies:
+        copy.wait()
 
 
 def on_device(conformations, fill_counts, dest_slots, dest_cells, velocity, noise):
@@ -446,7 +448,7 @@
     tile = velocity.shape
     arguments = (conformations, fill_counts, dest_slots, dest_cells, velocity, noise)
     dma = pltpu.SemaphoreType.DMA
-    return pl.pallas_call(
+    results = pl.pallas_call(
         kernel,
         out_shape=(
             pltpu.VMEM(noise.shape, F32),
@@ -466,8 +468,8 @@
             pltpu.VMEM((groups, 16, 2, 3, CAP, slots), F32),
             pltpu.VMEM((groups, 16, 2, 3, CAP, slots), F32),
             pltpu.VMEM((groups, 8, blocks), F32),
-            pltpu.VMEM((groups, 16, 2, 4, 128), F32),
-            pltpu.VMEM((groups, 16, 2, 4, 128), F32),
+            pltpu.VMEM((16, 2, 8, 128), F32),
+            pltpu.VMEM((16, 2, 8, 128), F32),
             pltpu.VMEM((groups, 16, 128, 16), F32),
             pltpu.VMEM((4,) + tile, F32),
             pltpu.VMEM((288, 128), BF16),
@@ -480,14 +482,21 @@
             pltpu.VMEM((4,) + tile, F32),
             pltpu.VMEM(tile, F32),
             dma((2,)), dma((4,)), dma,
-            dma((groups, 16, 2)), dma((groups, 16, 2)),
-            dma((groups, 16, 2)), dma((groups, 16, 2)),
+            dma((groups, 16, 2)), dma((groups, 16, 2)), dma((16, 2)), dma((16, 2)),
             dma((4,)), dma((4,)), dma((4,)), dma((4,)), dma((4,)), dma((4,)),
         ],
         compiler_params=pltpu.CompilerParams(
             collective_id=0, has_side_effects=True, vmem_limit_bytes=40 * 2**20
         ),
     )(*(pltpu.with_memory_space_constraint(x, pltpu.HBM) for x in arguments))
+    return pl.pallas_call(
+        finish,
+        out_shape=tuple(jax.ShapeDtypeStruct(x.shape, F32) for x in results),
+        in_specs=[vmem, vmem],
+        out_specs=(hbm, hbm),
+        scratch_shapes=[dma((7,))],
+        compiler_params=pltpu.CompilerParams(vmem_limit_bytes=2**20),
+    )(*(pltpu.with_memory_space_constraint(x, pltpu.VMEM) for x in results))
 
 
 def solution(mesh):

time: 75.2 us -> 71.5 us (0.951)
  local copies, waits for them, and re-layouts: 2.8 us -> 0 us
  Pallas kernels: 71.7 us -> 70.7 us
    pallas_call x1, Pallas kernels: 71.7 us -> 68.4 us  [on_device(): pl.pallas_call(kernel, out_shape=(pltpu.VMEM(noise.shape, F32), pltpu.VME...]
    unnamed x2 -> x0, local copies, waits for them, and re-layouts: 2.8 us -> none
    pallas_call x0 -> x1, Pallas kernels: none -> 2.24 us  [on_device(): pl.pallas_call(finish, out_shape=tuple((jax.ShapeDtypeStruct(x.shape, F32...]
where the time goes in v4:
time: 71.5 us; the launch traced here: 71.3 us
  Pallas kernels  70.7 us (99%)
    pallas_call x1, Pallas kernels, on_device(): pl.pallas_call(kernel, out_shape=(pltpu.VMEM(noise.shape, F32), pltpu.VME...  68.4 us
    pallas_call x1, Pallas kernels, on_device(): pl.pallas_call(finish, out_shape=tuple((jax.ShapeDtypeStruct(x.shape, F32...  2.24 us

profile of v4, /device:TPU:1, one launch (start us, length us, event | category | flops | bytes accessed | tf_op | source)
XLA Modules:
  0.0 71.3 jit_solution(10167900467987042776)
XLA Ops:
  0.6 68.4 %shard_map.77 = (f32[3,2,1536,128]{3,2,1,0:T(8,128)S(1)}, f32[3,8,256]{2,1,0:T(8,128)S(1)}) custom-call(f32[3,2,1024,128]{3,2,1,0:T(8,128)} %conf_hbm.1, s32[2,1024]{1,0:T(2,128)} %fill_hbm.1, s32[2,1024]{1,0:T(2,128)} %dest_hbm.1, s32[2,1024]{1,0:T(2,128)} %cell_hbm.1, f32[3,8,256]{2,1,0:T(8,128)} %vel_hbm.1, f32[3,2,1536,128]{3,2,1,0:T(8,128)} %noise_hbm.1), custom_call_target="tpu_custom_call" | custom-call | tf_op jit(solution)/shard_map/pallas_call | solution.py:451
  69.1 2.2 %shard_map.78 = (f32[3,2,1536,128]{3,2,1,0:T(8,128)}, f32[3,8,256]{2,1,0:T(8,128)}) custom-call(f32[3,2,1536,128]{3,2,1,0:T(8,128)S(1)} %get-tuple-element.4.conf_vmem, f32[3,8,256]{2,1,0:T(8,128)S(1)} %get-tuple-element.5.velocity_vmem), custom_call_target="tpu_custom_call" | custom-call | tf_op jit(solution)/shard_map/pallas_call | solution.py:492

commit v5 on v4

--- a/solution.py
+++ b/solution.py
@@ -125,7 +125,6 @@
     split(0)
     for copy in small:
         copy.wait()
-    pl.semaphore_wait(barrier, 31 + n_ens - 1)
 
     def vel_copy(slot, target):
         return pltpu.make_async_remote_copy(
@@ -134,13 +133,10 @@
         )
 
     halo_targets = (east_id, west_id, north_id, south_id)
-    for slot in range(4):
-        vel_copy(slot, halo_targets[slot]).start()
 
     def data_copy(g, i, p, r, h, target):
-        rows = pl.ds(h * PART, PART)
         return pltpu.make_async_remote_copy(
-            src_ref=sendbuf.at[g, i, r, :, rows], dst_ref=recv.at[g, p, r, :, rows],
+            src_ref=sendbuf.at[g, i, r, h], dst_ref=recv.at[g, p, r, h],
             send_sem=ssem.at[g, i, r], recv_sem=rsem.at[g, p, r],
             device_id=target, device_id_type=MESH,
         )
@@ -152,7 +148,7 @@
             device_id=target, device_id_type=MESH,
         )
 
-    def pack_batch(q, carry, g, width):
+    def pack_batch(q, carry, g, width, mode=3):
         code_x, code_z = carry
         targets, landing = [], []
         for _ in range(width):
@@ -162,6 +158,13 @@
             dz = jnp.where(core == 0, dz, lax.rem(4 - dz, 4))
             landing.append(dx * 4 + dz)
             targets += [chip(dx, dz, 0), chip(dx, dz, 1)]
+        if mode & 1:
+            fill_batch(q, g, width, targets)
+        if mode & 2:
+            start_batch(q, g, width, targets, landing)
+        return code_x, code_z
+
+    def fill_batch(q, g, width, targets):
         dest = dest_ref[g : g + 1, :]
         onehot = jnp.concatenate(
             [
@@ -174,11 +177,13 @@
             onehot, low[g], preferred_element_type=F32
         )
         for n in range(2 * width):
-            for a in range(3):
-                sendbuf[g, width * q + n // 2, n % 2, a] = packed[
-                    n * CAP : (n + 1) * CAP, a * 128 : (a + 1) * 128
-                ]
-
+            for h in range(HALVES):
+                for a in range(3):
+                    sendbuf[g, width * q + n // 2, n % 2, h, a] = packed[
+                        n * CAP + h * PART : n * CAP + (h + 1) * PART, a * 128 : (a + 1) * 128
+                    ]
+
+    def start_batch(q, g, width, targets, landing):
         def start(first, last):
             for h in range(HALVES):
                 for n in range(first, last):
@@ -195,16 +200,17 @@
             start(2 * width - 1, 2 * width)
             pltpu.make_async_copy(sendbuf.at[g, 15, 0], recv.at[g, 0, 0], rsem.at[g, 0, 0]).start()
 
-        return code_x, code_z
-
     codes = (jnp.int32(CODE_X), jnp.int32(CODE_Z))
 
-    def send_blocks(g, first, last, width=4):
+    def send_blocks(g, first, last, width=4, mode=3):
         start = tuple(jnp.int32(code // 4 ** (width * first)) for code in (CODE_X, CODE_Z))
-        lax.fori_loop(first, last, functools.partial(pack_batch, g=g, width=width), start)
-
-    send_blocks(0, 0, 2, width=2)
-    send_blocks(0, 1, 2)
+        lax.fori_loop(first, last, functools.partial(pack_batch, g=g, width=width, mode=mode), start)
+
+    send_blocks(0, 0, 2, mode=1)
+    pl.semaphore_wait(barrier, 31 + n_ens - 1)
+    for slot in range(4):
+        vel_copy(slot, halo_targets[slot]).start()
+    send_blocks(0, 0, 2, mode=2)
 
     lab_row = lax.broadcasted_iota(jnp.int32, (8, 128), 0)
     block_lane = lax.broadcasted_iota(jnp.int32, (128, 128), 1)
@@ -385,7 +391,12 @@
             rows = pl.ds(pl.multiple_of(source * CAP, CAP), CAP)
             here = columns[g, dx * 4 + dz, r * 64 : r * 64 + CAP]
             live = slot_lane < here[:, 9:10]
-            x = [jnp.where(live, recv[g, dx * 4 + dz, r, a], 0.0) for a in range(3)]
+            x = [
+                jnp.where(
+                    live, jnp.concatenate([recv[g, dx * 4 + dz, r, h, a] for h in range(HALVES)], axis=0), 0.0
+                )
+                for a in range(3)
+            ]
             inverse = 1.0 / (1.0 - (x[0] * x[0] + x[1] * x[1] + x[2] * x[2]) / EXTENSION)
             for a in range(3):
                 stretch = sum(here[:, 3 * a + b : 3 * a + b + 1] * x[b] for b in range(3))
@@ -465,8 +476,8 @@
             pltpu.VMEM(noise.shape, F32),
             pltpu.VMEM((groups, blocks, 3 * slots), BF16),
             pltpu.VMEM((groups, blocks, 3 * slots), BF16),
-            pltpu.VMEM((groups, 16, 2, 3, CAP, slots), F32),
-            pltpu.VMEM((groups, 16, 2, 3, CAP, slots), F32),
+            pltpu.VMEM((groups, 16, 2, HALVES, 3, PART, slots), F32),
+            pltpu.VMEM((groups, 16, 2, HALVES, 3, PART, slots), F32),
             pltpu.VMEM((groups, 8, blocks), F32),
             pltpu.VMEM((16, 2, 8, 128), F32),
             pltpu.VMEM((16, 2, 8, 128), F32),

time: 71.5 us -> 68.9 us (0.964)
  Pallas kernels: 70.7 us -> 68.2 us
    pallas_call x1, Pallas kernels: 68.4 us -> 65.9 us  [on_device(): pl.pallas_call(kernel, out_shape=(pltpu.VMEM(noise.shape, F32), pltpu.VME...]
where the time goes in v5:
time: 68.9 us; the launch traced here: 68.8 us
  Pallas kernels  68.2 us (99%)
    pallas_call x1, Pallas kernels, on_device(): pl.pallas_call(kernel, out_shape=(pltpu.VMEM(noise.shape, F32), pltpu.VME...  65.9 us
    pallas_call x1, Pallas kernels, on_device(): pl.pallas_call(finish, out_shape=tuple((jax.ShapeDtypeStruct(x.shape, F32...  2.24 us

profile of v5, /device:TPU:1, one launch (start us, length us, event | category | flops | bytes accessed | tf_op | source)
XLA Modules:
  0.0 68.8 jit_solution(2084154265450710053)
XLA Ops:
  0.6 65.9 %shard_map.77 = (f32[3,2,1536,128]{3,2,1,0:T(8,128)S(1)}, f32[3,8,256]{2,1,0:T(8,128)S(1)}) custom-call(f32[3,2,1024,128]{3,2,1,0:T(8,128)} %conf_hbm.1, s32[2,1024]{1,0:T(2,128)} %fill_hbm.1, s32[2,1024]{1,0:T(2,128)} %dest_hbm.1, s32[2,1024]{1,0:T(2,128)} %cell_hbm.1, f32[3,8,256]{2,1,0:T(8,128)} %vel_hbm.1, f32[3,2,1536,128]{3,2,1,0:T(8,128)} %noise_hbm.1), custom_call_target="tpu_custom_call" | custom-call | tf_op jit(solution)/shard_map/pallas_call | solution.py:462
  66.6 2.2 %shard_map.78 = (f32[3,2,1536,128]{3,2,1,0:T(8,128)}, f32[3,8,256]{2,1,0:T(8,128)}) custom-call(f32[3,2,1536,128]{3,2,1,0:T(8,128)S(1)} %get-tuple-element.4.conf_vmem, f32[3,8,256]{2,1,0:T(8,128)S(1)} %get-tuple-element.5.velocity_vmem), custom_call_target="tpu_custom_call" | custom-call | tf_op jit(solution)/shard_map/pallas_call | solution.py:503

commit v6 on v5

--- a/solution.py
+++ b/solution.py
@@ -65,7 +65,7 @@
 def kernel(
     conf_hbm, fill_hbm, dest_hbm, cell_hbm, vel_hbm, noise_hbm,
     out_ref, vout_ref,
-    conf, fill_ref, dest_ref, cell_ref, vel_ref, noise, high, low, sendbuf, recv, labels, labsend, labrecv, columns,
+    conf, fill_ref, dest_ref, cell_ref, vel_ref, noise, terms, sendbuf, recv, labels, labsend, labrecv, columns,
     vhalo, table, rowbuf, field, sx, sy, shx, shy, dv, base,
     conf_sem, in_sem, noise_sem, ssem, rsem, lssem, lrsem, vs_sem, vr_sem, hs_sem, hr_sem, ds_sem, dr_sem,
 ):
@@ -76,8 +76,8 @@
     core = lax.rem(cx, 2)
     n_ens = 4
 
-    def conf_copy(g):
-        return pltpu.make_async_copy(conf_hbm.at[:, g], conf.at[:, g], conf_sem.at[g])
+    def conf_copy(g, a):
+        return pltpu.make_async_copy(conf_hbm.at[a, g], conf.at[a, g], conf_sem.at[g, a])
 
     small = [
         pltpu.make_async_copy(source, target, in_sem.at[k])
@@ -85,7 +85,8 @@
             ((dest_hbm, dest_ref), (vel_hbm, vel_ref), (fill_hbm, fill_ref), (cell_hbm, cell_ref))
         )
     ]
-    conf_copy(0).start()
+    for a in range(3):
+        conf_copy(0, a).start()
     for copy in small:
         copy.start()
     noise_copy = pltpu.make_async_copy(noise_hbm, noise, noise_sem)
@@ -110,9 +111,12 @@
 
     def split(g):
         for a in range(3):
+            if g == 0:
+                conf_copy(0, a).wait()
+                conf_copy(1, a).start()
             first, second = halves_of(conf[a, g])
-            high[g, :, a * 128 : (a + 1) * 128] = first
-            low[g, :, a * 128 : (a + 1) * 128] = second
+            terms[g, :, a * 128 : (a + 1) * 128] = first
+            terms[g, :, (a + 3) * 128 : (a + 4) * 128] = second
 
     blocks = conf.shape[2]
     row48 = lax.broadcasted_iota(jnp.int32, (CAP, blocks), 0)
@@ -120,15 +124,16 @@
 
     field[...] = jnp.zeros_like(field)
     rowbuf[...] = jnp.zeros_like(rowbuf)
-    conf_copy(0).wait()
-    conf_copy(1).start()
     split(0)
     for copy in small:
         copy.wait()
 
+    def lanes_of(slot):
+        return pl.ds(0, 256) if slot < 2 else pl.ds(128, 128) if slot == 2 else pl.ds(0, 128)
+
     def vel_copy(slot, target):
         return pltpu.make_async_remote_copy(
-            src_ref=vel_ref, dst_ref=vhalo.at[slot], send_sem=vs_sem.at[slot], recv_sem=vr_sem.at[slot],
+            src_ref=vel_ref.at[:, :, lanes_of(slot)], dst_ref=vhalo.at[slot, :, :, lanes_of(slot)], send_sem=vs_sem.at[slot], recv_sem=vr_sem.at[slot],
             device_id=target, device_id_type=MESH,
         )
 
@@ -173,9 +178,8 @@
             ],
             axis=0,
         )
-        packed = jnp.dot(onehot, high[g], preferred_element_type=F32) + jnp.dot(
-            onehot, low[g], preferred_element_type=F32
-        )
+        packed = jnp.dot(onehot, terms[g], preferred_element_type=F32)
+        packed = packed[:, :384] + packed[:, 384:]
         for n in range(2 * width):
             for h in range(HALVES):
                 for a in range(3):
@@ -231,10 +235,15 @@
         labels[g, :, rows] = jnp.where(lab_row == 0, fill, jnp.where(lab_row == 1, cell, sums))
         return carry
 
-    conf_copy(1).wait()
+    for a in range(3):
+        conf_copy(1, a).wait()
     noise_copy.start()
-    for g in range(2):
-        lax.fori_loop(0, blocks // 128, functools.partial(label_rows, g=g), 0)
+    def both_rows(k, carry):
+        for g in range(2):
+            label_rows(k, carry, g)
+        return carry
+
+    lax.fori_loop(0, blocks // 128, both_rows, 0)
 
     row128 = lax.broadcasted_iota(jnp.int32, (128, blocks), 0)
 
@@ -355,8 +364,10 @@
         dv[ens, k] = 0.5 * (u - d)
 
     def stress_copy(slot):
+        lanes = lanes_of(slot)
         return pltpu.make_async_remote_copy(
-            src_ref=sx if slot < 2 else sy, dst_ref=shx.at[slot] if slot < 2 else shy.at[slot - 2],
+            src_ref=(sx if slot < 2 else sy).at[:, :, lanes],
+            dst_ref=(shx.at[slot] if slot < 2 else shy.at[slot - 2]).at[:, :, lanes],
             send_sem=hs_sem.at[slot], recv_sem=hr_sem.at[slot],
             device_id=halo_targets[slot], device_id_type=MESH,
         )
@@ -474,8 +485,7 @@
             pltpu.VMEM(fill_counts.shape, jnp.int32),
             pltpu.VMEM(tile, F32),
             pltpu.VMEM(noise.shape, F32),
-            pltpu.VMEM((groups, blocks, 3 * slots), BF16),
-            pltpu.VMEM((groups, blocks, 3 * slots), BF16),
+            pltpu.VMEM((groups, blocks, 6 * slots), BF16),
             pltpu.VMEM((groups, 16, 2, HALVES, 3, PART, slots), F32),
             pltpu.VMEM((groups, 16, 2, HALVES, 3, PART, slots), F32),
             pltpu.VMEM((groups, 8, blocks), F32),
@@ -492,7 +502,7 @@
             pltpu.VMEM((2,) + tile, F32),
             pltpu.VMEM((4,) + tile, F32),
             pltpu.VMEM(tile, F32),
-            dma((2,)), dma((4,)), dma,
+            dma((2, 3)), dma((4,)), dma,
             dma((groups, 16, 2)), dma((groups, 16, 2)), dma((16, 2)), dma((16, 2)),
             dma((4,)), dma((4,)), dma((4,)), dma((4,)), dma((4,)), dma((4,)),
         ],

time: 68.9 us -> 69 us (level)
  no operation moved by 1% of the time
where the time goes in v6:
time: 69 us; the launch traced here: 68.9 us
  Pallas kernels  68.2 us (99%)
    pallas_call x1, Pallas kernels, on_device(): pl.pallas_call(kernel, out_shape=(pltpu.VMEM(noise.shape, F32), pltpu.VME...  66 us
    pallas_call x1, Pallas kernels, on_device(): pl.pallas_call(finish, out_shape=tuple((jax.ShapeDtypeStruct(x.shape, F32...  2.24 us

profile of v6, /device:TPU:1, one launch (start us, length us, event | category | flops | bytes accessed | tf_op | source)
XLA Modules:
  0.0 68.9 jit_solution(12202406729523055090)
XLA Ops:
  0.6 66.0 %shard_map.77 = (f32[3,2,1536,128]{3,2,1,0:T(8,128)S(1)}, f32[3,8,256]{2,1,0:T(8,128)S(1)}) custom-call(f32[3,2,1024,128]{3,2,1,0:T(8,128)} %conf_hbm.1, s32[2,1024]{1,0:T(2,128)} %fill_hbm.1, s32[2,1024]{1,0:T(2,128)} %dest_hbm.1, s32[2,1024]{1,0:T(2,128)} %cell_hbm.1, f32[3,8,256]{2,1,0:T(8,128)} %vel_hbm.1, f32[3,2,1536,128]{3,2,1,0:T(8,128)} %noise_hbm.1), custom_call_target="tpu_custom_call" | custom-call | tf_op jit(solution)/shard_map/pallas_call | solution.py:473
  66.6 2.2 %shard_map.78 = (f32[3,2,1536,128]{3,2,1,0:T(8,128)}, f32[3,8,256]{2,1,0:T(8,128)}) custom-call(f32[3,2,1536,128]{3,2,1,0:T(8,128)S(1)} %get-tuple-element.4.conf_vmem, f32[3,8,256]{2,1,0:T(8,128)S(1)} %get-tuple-element.5.velocity_vmem), custom_call_target="tpu_custom_call" | custom-call | tf_op jit(solution)/shard_map/pallas_call | solution.py:513

commit v7 on v6

--- a/solution.py
+++ b/solution.py
@@ -128,12 +128,9 @@
     for copy in small:
         copy.wait()
 
-    def lanes_of(slot):
-        return pl.ds(0, 256) if slot < 2 else pl.ds(128, 128) if slot == 2 else pl.ds(0, 128)
-
     def vel_copy(slot, target):
         return pltpu.make_async_remote_copy(
-            src_ref=vel_ref.at[:, :, lanes_of(slot)], dst_ref=vhalo.at[slot, :, :, lanes_of(slot)], send_sem=vs_sem.at[slot], recv_sem=vr_sem.at[slot],
+            src_ref=vel_ref, dst_ref=vhalo.at[slot], send_sem=vs_sem.at[slot], recv_sem=vr_sem.at[slot],
             device_id=target, device_id_type=MESH,
         )
 
@@ -238,12 +235,8 @@
     for a in range(3):
         conf_copy(1, a).wait()
     noise_copy.start()
-    def both_rows(k, carry):
-        for g in range(2):
-            label_rows(k, carry, g)
-        return carry
-
-    lax.fori_loop(0, blocks // 128, both_rows, 0)
+    for g in range(2):
+        lax.fori_loop(0, blocks // 128, functools.partial(label_rows, g=g), 0)
 
     row128 = lax.broadcasted_iota(jnp.int32, (128, blocks), 0)
 
@@ -364,10 +357,8 @@
         dv[ens, k] = 0.5 * (u - d)
 
     def stress_copy(slot):
-        lanes = lanes_of(slot)
         return pltpu.make_async_remote_copy(
-            src_ref=(sx if slot < 2 else sy).at[:, :, lanes],
-            dst_ref=(shx.at[slot] if slot < 2 else shy.at[slot - 2]).at[:, :, lanes],
+            src_ref=sx if slot < 2 else sy, dst_ref=shx.at[slot] if slot < 2 else shy.at[slot - 2],
             send_sem=hs_sem.at[slot], recv_sem=hr_sem.at[slot],
             device_id=halo_targets[slot], device_id_type=MESH,
         )

time: 69 us -> 69 us (level)
  no operation moved by 1% of the time
where the time goes in v7:
time: 69 us; the launch traced here: 68.8 us
  Pallas kernels  68.2 us (99%)
    pallas_call x1, Pallas kernels, on_device(): pl.pallas_call(kernel, out_shape=(pltpu.VMEM(noise.shape, F32), pltpu.VME...  66 us
    pallas_call x1, Pallas kernels, on_device(): pl.pallas_call(finish, out_shape=tuple((jax.ShapeDtypeStruct(x.shape, F32...  2.24 us

profile of v7, /device:TPU:1, one launch (start us, length us, event | category | flops | bytes accessed | tf_op | source)
XLA Modules:
  0.0 68.8 jit_solution(5978989813440411635)
XLA Ops:
  0.6 66.0 %shard_map.77 = (f32[3,2,1536,128]{3,2,1,0:T(8,128)S(1)}, f32[3,8,256]{2,1,0:T(8,128)S(1)}) custom-call(f32[3,2,1024,128]{3,2,1,0:T(8,128)} %conf_hbm.1, s32[2,1024]{1,0:T(2,128)} %fill_hbm.1, s32[2,1024]{1,0:T(2,128)} %dest_hbm.1, s32[2,1024]{1,0:T(2,128)} %cell_hbm.1, f32[3,8,256]{2,1,0:T(8,128)} %vel_hbm.1, f32[3,2,1536,128]{3,2,1,0:T(8,128)} %noise_hbm.1), custom_call_target="tpu_custom_call" | custom-call | tf_op jit(solution)/shard_map/pallas_call | solution.py:464
  66.6 2.2 %shard_map.78 = (f32[3,2,1536,128]{3,2,1,0:T(8,128)}, f32[3,8,256]{2,1,0:T(8,128)}) custom-call(f32[3,2,1536,128]{3,2,1,0:T(8,128)S(1)} %get-tuple-element.4.conf_vmem, f32[3,8,256]{2,1,0:T(8,128)S(1)} %get-tuple-element.5.velocity_vmem), custom_call_target="tpu_custom_call" | custom-call | tf_op jit(solution)/shard_map/pallas_call | solution.py:504
